TPU v7x, 256 devices: a whole 4x4x8 slice. The times are simulated.
256 devices in a mesh: dp: 4 (over y), expert: 64 (over z, x, core).
Axes of the slice: x: 4, y: 4, z: 8, core: 2. Of those that a mesh axis runs over, the one named last changes fastest.
Arguments:
- layer_inputs: bfloat16 [32768, 2048], P(('dp', 'expert')), may hold values from -6 to 6
- output_adjoint: bfloat16 [32768, 2048], P(('dp', 'expert')), may hold values from -6 to 6
- dispatcher_projection: bfloat16 [2048, 64], replicated, may hold values from -0.25 to 0.25
- gating_kernel: bfloat16 [2048, 128, 384], P('dp', 'expert'), may hold values from -0.125 to 0.125
- expansion_kernel: bfloat16 [2048, 128, 384], P('dp', 'expert'), may hold values from -0.125 to 0.125
- contraction_kernel: bfloat16 [2048, 128, 384], P('dp', 'expert'), may hold values from -0.3125 to 0.3125
- token_experts: int32 [32768, 8], P(('dp', 'expert')), may hold values from 0 to 63, all different within a row
- copy_choice_index: int32 [32768, 8], P(('dp', 'expert')), may hold values from 0 to 3
- expert_copies: int32 [64, 4], replicated, may hold values from 0 to 127, as said below
- send_quotas: int32 [128], replicated, may hold values from 3 to 5, as said below
Outputs:
- token_grad: bfloat16 [32768, 2048], P(('dp', 'expert'))
- gate_grad: float32 [2048, 128, 384], P('dp', 'expert')
- up_grad: float32 [2048, 128, 384], P('dp', 'expert')
- down_grad: float32 [2048, 128, 384], P('dp', 'expert')
- router_grad: float32 [2048, 64], P('dp', 'expert')
Inputs may be any that keep to these rules, and one draw needn't show every extreme that they name: `expert_copies`: row e lists slots that hold expert e, repeats allowed, starting with slot e * 2; every slot appears in exactly one row. `send_quotas`: some slot has capacity exactly 5.
All inputs are finite; a program needn't handle non-finite values.
Results may differ from a plain program's by a relative error of at most 0.017.
Values may be sent and summed in bfloat16 or wider, within the bound.
A program may use at most 128 MiB of HBM per device.

v0:
```python
import functools

import jax
import jax.numpy as jnp
from jax import lax
from jax.experimental import pallas as pl
from jax.experimental.pallas import tpu as pltpu
from jax.sharding import PartitionSpec as P

CAP = 5
LANES = 128
MESH = pl.DeviceIdType.MESH
F32 = jnp.float32
BF16 = jnp.bfloat16


def dispatch_kernel(pick, x_ref, g_ref, out_ref, flat):
    tokens, width = x_ref.shape
    slabs = width // LANES
    slots, devs, depth = out_ref.shape[:3]
    cap = depth // 2
    flat[pl.ds(tokens * slabs, slabs), :] = jnp.zeros((slabs, LANES), F32)
    for which, ref in enumerate((x_ref, g_ref)):
        for a in range(slabs):
            flat[pl.ds(a, tokens, stride=slabs), :] = ref[:, a * LANES : (a + 1) * LANES].astype(F32)

        def one(d, carry, which=which):
            for s in range(slots):
                for c in range(cap):
                    token = pick[(s * devs + d) * cap + c]
                    row = pl.multiple_of(token * slabs, slabs)
                    out_ref[s, d, which * cap + c] = flat[pl.ds(row, slabs), :].astype(BF16)
            return carry

        lax.fori_loop(0, devs, one, 0)


def combine_kernel(place, back_ref, lg_ref, proj_ref, out_ref, flat):
    tokens, width = out_ref.shape
    slabs = width // LANES
    fanout = place.shape[0] // tokens

    def one(t, carry):
        total = back_ref[place[t * fanout]].astype(F32)
        for k in range(1, fanout):
            total = total + back_ref[place[t * fanout + k]].astype(F32)
        flat[pl.ds(pl.multiple_of(t * slabs, slabs), slabs), :] = total
        return carry

    lax.fori_loop(0, tokens, one, 0)
    for a in range(slabs):
        cols = slice(a * LANES, (a + 1) * LANES)
        routed = lax.dot_general(
            lg_ref[...], proj_ref[cols, :], (((1,), (1,)), ((), ())), preferred_element_type=F32
        )
        out_ref[:, cols] = (flat[pl.ds(a, tokens, stride=slabs), :] + routed).astype(BF16)


def exchange_kernel(
    n_dp,
    n_exp,
    send,
    q_send,
    w,
    x,
    te,
    dev,
    lane,
    probs,
    back,
    dw,
    lg_out,
    rcol,
    recv,
    q_recv,
    wf,
    flat,
    xm,
    gm,
    gu,
    act_s,
    dwp,
    rs1,
    rs2,
    dxs,
    zero,
    pg,
    pg_recv,
    rt,
    rt_recv,
    r2,
    tok_ss,
    tok_rs,
    q_ss,
    q_rs,
    w_ss,
    w_rs,
    g_ss,
    g_rs,
    dx_ss,
    dx_rs,
    pg_ss,
    pg_rs,
    rt_ss,
    rt_rs,
    r2_ss,
    r2_rs,
    own_sem,
):
    me = lax.axis_index("expert")
    my = lax.axis_index("dp")
    right = lax.rem(my + 1, n_dp)
    far = lax.rem(my + 2, n_dp)
    left = lax.rem(my + 3, n_dp)
    slots, _, depth, slabs, _ = recv.shape
    cap = depth // 2
    rows = cap * n_exp
    quarter = wf.shape[2]
    half = quarter // 2
    ff = wf.shape[3] // 3
    per = slabs // n_dp
    chunk = min(8, n_exp)
    others = n_exp - 1

    barrier = pltpu.get_barrier_semaphore()

    def greet(i, carry):
        pl.semaphore_signal(
            barrier, inc=1, device_id={"expert": lax.rem(me + i, n_exp)}, device_id_type=MESH
        )
        return carry

    lax.fori_loop(1, n_exp, greet, 0)
    for other in (right, far, left):
        pl.semaphore_signal(barrier, inc=1, device_id={"dp": other}, device_id_type=MESH)
    pl.semaphore_wait(barrier, others + n_dp - 1)

    def to_dp(src, dst, ss, rs, other):
        return pltpu.make_async_remote_copy(
            src, dst, ss, rs, device_id={"dp": other}, device_id_type=MESH
        )

    def to_exp(src, dst, ss, rs, other):
        return pltpu.make_async_remote_copy(
            src, dst, ss, rs, device_id={"expert": other}, device_id_type=MESH
        )

    def to_all(make):
        def one(i, carry):
            make(lax.rem(me + i, n_exp)).start()
            return carry

        lax.fori_loop(1, n_exp, one, 0)

    def wait_for(ref, sem):
        pltpu.make_async_copy(ref, ref, sem).wait()

    def w_first(s):
        for n, other in enumerate((right, left)):
            to_dp(w.at[s], wf.at[s, my], w_ss.at[s, n], w_rs.at[s, n], other).start()

    def w_second(s):
        wait_for(wf.at[s, left], w_rs.at[s, 0])
        part = wf.at[s, left, pl.ds(0, half)]
        to_dp(part, part, w_ss.at[s, 2], w_rs.at[s, 2], right).start()
        wait_for(wf.at[s, right], w_rs.at[s, 1])
        part = wf.at[s, right, pl.ds(half, half)]
        to_dp(part, part, w_ss.at[s, 3], w_rs.at[s, 3], left).start()

    def w_end(s):
        wait_for(wf.at[s, far, pl.ds(0, half)], w_rs.at[s, 2])
        wait_for(wf.at[s, far, pl.ds(half, half)], w_rs.at[s, 3])

    w_first(0)
    own = [pltpu.make_async_copy(w.at[s], wf.at[s, my], own_sem.at[s]) for s in range(slots)]
    own += [
        pltpu.make_async_copy(send.at[s, me], recv.at[s, me], own_sem.at[slots + s])
        for s in range(slots)
    ]
    for copy in own:
        copy.start()
    to_all(lambda d: to_exp(send.at[0, d], recv.at[0, me], tok_ss.at[0], tok_rs.at[0], d))
    to_all(lambda d: to_exp(q_send.at[d], q_recv.at[me], q_ss, q_rs, d))
    to_all(lambda d: to_exp(send.at[1, d], recv.at[1, me], tok_ss.at[1], tok_rs.at[1], d))
    q_recv[me] = q_send[me]
    zero[...] = jnp.zeros_like(zero)
    zero_copy = pltpu.make_async_copy(zero, back.at[slots * rows], own_sem.at[2 * slots])
    zero_copy.start()
    w_second(0)
    w_first(1)

    def to_matrix(s, which, out):
        def unpack(i, carry):
            block = recv[s, pl.ds(i * chunk, chunk), which * cap : (which + 1) * cap]
            size = chunk * cap * slabs
            flat[pl.ds(pl.multiple_of(i * size, size), size), :] = block.astype(F32).reshape(
                size, LANES
            )
            return carry

        lax.fori_loop(0, n_exp // chunk, unpack, 0)

        def gather(p, carry):
            for b in range(per):
                for c in range(cap):
                    part = flat[pl.ds(c * slabs + p * per + b, n_exp, stride=cap * slabs), :]
                    out[p, c * n_exp : (c + 1) * n_exp, b * LANES : (b + 1) * LANES] = part.astype(
                        BF16
                    )
            return carry

        lax.fori_loop(0, n_dp, gather, 0)

    lanes = lax.broadcasted_iota(jnp.int32, (n_exp, LANES), 1)

    def weight_of(s):
        table = q_recv[...].reshape(n_exp, LANES)
        return jnp.concatenate(
            [table[:, s * cap + c : s * cap + c + 1] for c in range(cap)], axis=0
        )

    def forward(s):
        to_matrix(s, 0, xm)
        to_matrix(s, 1, gm)

        def project(p, carry):
            gate_up, down = carry
            gate_up = gate_up + jnp.dot(
                xm[p], wf[s, p, :, : 2 * ff], preferred_element_type=F32
            )
            down = down + jnp.dot(gm[p], wf[s, p, :, 2 * ff :], preferred_element_type=F32)
            return gate_up, down

        gate_up, down = lax.fori_loop(
            0, n_dp, project, (jnp.zeros((rows, 2 * ff), F32), jnp.zeros((rows, ff), F32))
        )
        gate, up = gate_up[:, :ff], gate_up[:, ff:]
        sig = jax.nn.sigmoid(gate)
        silu = gate * sig
        act = (silu * up).astype(BF16)
        act_s[...] = act
        grad = jnp.sum(act.astype(F32) * down, axis=1, keepdims=True).astype(BF16).astype(F32)
        act_grad = weight_of(s) * down
        gu[:, :ff] = (act_grad * up * sig * (1.0 + gate * (1.0 - sig))).astype(BF16)
        gu[:, ff:] = (act_grad * silu).astype(BF16)
        table = jnp.zeros((n_exp, LANES), F32)
        for c in range(cap):
            table = jnp.where(
                lanes == s * cap + c, grad[c * n_exp : (c + 1) * n_exp], table
            )
        return table

    def weight_grad(s, p):
        both = (((0,), (0,)), ((), ()))
        dwp[s, p, :, : 2 * ff] = lax.dot_general(
            xm[p], gu[...], both, preferred_element_type=F32
        ).astype(BF16)
        out_grad = (weight_of(s) * gm[p].astype(F32)).astype(BF16)
        dwp[s, p, :, 2 * ff :] = lax.dot_general(
            out_grad, act_s[...], both, preferred_element_type=F32
        ).astype(BF16)

    def input_grad(s):
        def one(p, carry):
            value = lax.dot_general(
                gu[...],
                wf[s, p, :, : 2 * ff],
                (((1,), (1,)), ((), ())),
                preferred_element_type=F32,
            )
            for b in range(per):
                for c in range(cap):
                    flat[pl.ds(c * slabs + p * per + b, n_exp, stride=cap * slabs), :] = value[
                        c * n_exp : (c + 1) * n_exp, b * LANES : (b + 1) * LANES
                    ]
            return carry

        lax.fori_loop(0, n_dp, one, 0)

        def pack(i, carry):
            size = chunk * cap * slabs
            block = flat[pl.ds(pl.multiple_of(i * size, size), size), :]
            dxs[s, pl.ds(i * chunk, chunk)] = block.astype(BF16).reshape(chunk, cap, slabs, LANES)
            return carry

        lax.fori_loop(0, n_exp // chunk, pack, 0)

    def place(s, d):
        return back.at[pl.ds((s * n_exp + d) * cap, cap)]

    def dx_start(s):
        pltpu.make_async_copy(dxs.at[s, me], place(s, me), own_sem.at[2 * slots + 1 + s]).start()
        to_all(lambda d: to_exp(dxs.at[s, d], place(s, me), dx_ss.at[s], dx_rs.at[s], d))

    def sum_first(s):
        to_dp(
            dwp.at[s, far, pl.ds(0, half)], rs1.at[s, 0], g_ss.at[s, 0], g_rs.at[s, 0], right
        ).start()
        to_dp(
            dwp.at[s, far, pl.ds(half, half)], rs1.at[s, 1], g_ss.at[s, 1], g_rs.at[s, 1], left
        ).start()

    def sum_second(s):
        for n, other in enumerate((right, left)):
            wait_for(rs1.at[s, n], g_rs.at[s, n])
            part = pl.ds(n * half, half)
            dwp[s, other, part] = (
                dwp[s, other, part].astype(F32) + rs1[s, n].astype(F32)
            ).astype(BF16)
            to_dp(
                dwp.at[s, other], rs2.at[s, n], g_ss.at[s, 2 + n], g_rs.at[s, 2 + n], other
            ).start()

    def sum_end(s):
        wait_for(rs2.at[s, 0], g_rs.at[s, 2])
        wait_for(rs2.at[s, 1], g_rs.at[s, 3])
        dw[s] = dwp[s, my].astype(F32) + rs2[s, 0].astype(F32) + rs2[s, 1].astype(F32)

    def tokens_here(s):
        wait_for(recv.at[s, pl.ds(0, others)], tok_rs.at[s])
        own[slots + s].wait()

    tokens_here(0)
    wait_for(q_recv.at[pl.ds(0, others)], q_rs)
    own[0].wait()
    w_end(0)
    table = forward(0)
    weight_grad(0, far)
    sum_first(0)
    w_second(1)
    weight_grad(0, right)
    weight_grad(0, left)
    weight_grad(0, my)
    input_grad(0)
    sum_second(0)
    own[1].wait()
    w_end(1)

    tokens_here(1)
    dx_start(0)
    table = table + forward(1)
    pg[...] = table.reshape(pg.shape)
    to_all(lambda d: to_exp(pg.at[d], pg_recv.at[me], pg_ss, pg_rs, d))
    pg_recv[me] = pg[me]
    weight_grad(1, far)
    sum_first(1)
    weight_grad(1, right)
    weight_grad(1, left)
    weight_grad(1, my)
    input_grad(1)
    dx_start(1)
    sum_second(1)

    wait_for(pg_recv.at[pl.ds(0, others)], pg_rs)
    grads = pg_recv[...].reshape(n_exp, LANES).astype(BF16)
    tokens, fanout = te.shape
    dev_ids = lax.broadcasted_iota(jnp.int32, (tokens, n_exp), 1)
    lane_ids = lax.broadcasted_iota(jnp.int32, (tokens, LANES), 1)
    pair = []
    weighted = jnp.zeros((tokens, 1), F32)
    for k in range(fanout):
        hit = (dev[:, k : k + 1] == dev_ids).astype(F32).astype(BF16)
        spread = jnp.dot(hit, grads, preferred_element_type=F32)
        value = jnp.sum(
            jnp.where(lane[:, k : k + 1] == lane_ids, spread, 0.0), axis=1, keepdims=True
        )
        pair.append(value)
        weighted = weighted + probs[:, k : k + 1] * value
    logit = jnp.zeros((tokens, n_exp), F32)
    for k in range(fanout):
        chosen = probs[:, k : k + 1] * (pair[k] - weighted)
        logit = logit + jnp.where(te[:, k : k + 1] == dev_ids, chosen, 0.0)
    logit = logit.astype(BF16)
    lg_out[...] = logit
    for a in range(slabs):
        flat[pl.ds(a, n_exp, stride=slabs), :] = lax.dot_general(
            logit,
            x[:, a * LANES : (a + 1) * LANES],
            (((0,), (0,)), ((), ())),
            preferred_element_type=F32,
        )
    rt[...] = flat[pl.ds(0, n_exp * slabs), :].astype(BF16).reshape(rt.shape)
    to_all(lambda d: to_exp(rt.at[d], rt_recv.at[me], rt_ss, rt_rs, d))
    rt_recv[me] = rt[me]
    sum_end(0)
    wait_for(rt_recv.at[pl.ds(0, others)], rt_rs)
    r2[0] = jnp.sum(rt_recv[...].astype(F32), axis=0)
    for n, other in enumerate((right, far, left)):
        to_dp(r2.at[0], r2.at[n + 1], r2_ss.at[n], r2_rs.at[n], other).start()
    for n in range(n_dp - 1):
        wait_for(r2.at[n + 1], r2_rs.at[n])
    rcol[...] = r2[0] + r2[1] + r2[2] + r2[3]
    sum_end(1)

    zero_copy.wait()
    wait_for(q_send.at[pl.ds(0, others)], q_ss)
    wait_for(pg.at[pl.ds(0, others)], pg_ss)
    wait_for(rt.at[pl.ds(0, others)], rt_ss)
    for n in range(n_dp - 1):
        wait_for(r2.at[0], r2_ss.at[n])
    for s in range(slots):
        wait_for(recv.at[s, pl.ds(0, others)], tok_ss.at[s])
        wait_for(wf.at[s, 0], w_ss.at[s, 0])
        wait_for(wf.at[s, 0], w_ss.at[s, 1])
        for n in (2, 3):
            wait_for(wf.at[s, 0, pl.ds(0, half)], w_ss.at[s, n])
        for n in (0, 1):
            wait_for(rs1.at[s, n], g_ss.at[s, n])
            wait_for(rs2.at[s, n], g_ss.at[s, 2 + n])
        pltpu.make_async_copy(dxs.at[s, me], place(s, me), own_sem.at[2 * slots + 1 + s]).wait()
        wait_for(dxs.at[s, pl.ds(0, others)], dx_ss.at[s])
        wait_for(dxs.at[s, pl.ds(0, others)], dx_rs.at[s])


def exchange(n_dp, n_exp, send, q_send, w, x, te, dev, lane, probs):
    slots, _, depth, slabs, _ = send.shape
    cap = depth // 2
    rows = cap * n_exp
    quarter, wide = w.shape[1:]
    half = quarter // 2
    ff = wide // 3
    tokens = x.shape[0]
    vmem = pl.BlockSpec(memory_space=pltpu.VMEM)
    hbm = pl.BlockSpec(memory_space=pl.ANY)
    dma = pltpu.SemaphoreType.DMA
    return pl.pallas_call(
        functools.partial(exchange_kernel, n_dp, n_exp),
        out_shape=(
            jax.ShapeDtypeStruct((slots * rows + 1, slabs, LANES), BF16),
            jax.ShapeDtypeStruct((slots, quarter, wide), F32),
            jax.ShapeDtypeStruct((tokens, n_exp), BF16),
            jax.ShapeDtypeStruct((slabs, LANES), F32),
        ),
        in_specs=[hbm, vmem, hbm, vmem, vmem, vmem, vmem, vmem],
        out_specs=(hbm, vmem, vmem, vmem),
        scratch_shapes=[
            pltpu.VMEM(send.shape, BF16),
            pltpu.VMEM((n_exp, 1, LANES), F32),
            pltpu.VMEM((slots, n_dp, quarter, wide), BF16),
            pltpu.VMEM((rows * slabs, LANES), F32),
            pltpu.VMEM((n_dp, rows, quarter), BF16),
            pltpu.VMEM((n_dp, rows, quarter), BF16),
            pltpu.VMEM((rows, 2 * ff), BF16),
            pltpu.VMEM((rows, ff), BF16),
            pltpu.VMEM((slots, n_dp, quarter, wide), BF16),
            pltpu.VMEM((slots, 2, half, wide), BF16),
            pltpu.VMEM((slots, 2, quarter, wide), BF16),
            pltpu.VMEM((slots, n_exp, cap, slabs, LANES), BF16),
            pltpu.VMEM((slabs, LANES), BF16),
            pltpu.VMEM((n_exp, 1, LANES), F32),
            pltpu.VMEM((n_exp, 1, LANES), F32),
            pltpu.VMEM((n_exp, slabs, LANES), BF16),
            pltpu.VMEM((n_exp, slabs, LANES), BF16),
            pltpu.VMEM((n_dp, slabs, LANES), F32),
            dma((slots,)),
            dma((slots,)),
            dma,
            dma,
            dma((slots, 4)),
            dma((slots, 4)),
            dma((slots, 4)),
            dma((slots, 4)),
            dma((slots,)),
            dma((slots,)),
            dma,
            dma,
            dma,
            dma,
            dma((n_dp - 1,)),
            dma((n_dp - 1,)),
            dma((3 * slots + 1,)),
        ],
        compiler_params=pltpu.CompilerParams(
            collective_id=0, has_side_effects=True, vmem_limit_bytes=60 * 1024 * 1024
        ),
    )(send, q_send, w, x, te, dev, lane, probs)


def shards(
    n_dp,
    n_exp,
    layer_inputs,
    output_adjoint,
    dispatcher_projection,
    gating_kernel,
    expansion_kernel,
    contraction_kernel,
    token_experts,
    copy_choice_index,
    expert_copies,
    send_quotas,
):
    tokens, width = layer_inputs.shape
    fanout = token_experts.shape[1]
    experts = dispatcher_projection.shape[1]
    replicas = expert_copies.shape[1]
    position_count = send_quotas.shape[0]
    slots = gating_kernel.shape[1]
    hidden = gating_kernel.shape[2]
    slabs = width // LANES
    pairs = tokens * fanout
    sent = slots * n_exp * CAP

    logits = jnp.dot(layer_inputs, dispatcher_projection, preferred_element_type=F32)
    route_hit = token_experts[:, :, None] == lax.iota(jnp.int32, experts)[None, None, :]
    chosen = jnp.sum(jnp.where(route_hit, logits[:, None, :], 0.0), axis=2)
    probs = jax.nn.softmax(chosen, axis=1)
    flat_pick = (token_experts * replicas + copy_choice_index).reshape(pairs)
    target = jnp.sum(
        jnp.where(
            flat_pick[:, None] == lax.iota(jnp.int32, experts * replicas)[None, :],
            expert_copies.reshape(experts * replicas)[None, :],
            0,
        ),
        axis=1,
    )
    agrees = (target[:, None] == lax.iota(jnp.int32, position_count)[None, :]).astype(jnp.int32)
    arrival = jnp.sum((jnp.cumsum(agrees, axis=0) - agrees) * agrees, axis=1)
    bound = jnp.sum(agrees * send_quotas[None, :], axis=1)
    kept = arrival < bound
    owner = target // slots
    local = target % slots
    position = jnp.where(kept, (local * n_exp + owner) * CAP + arrival, sent)
    hit = position[None, :] == lax.iota(jnp.int32, sent)[:, None]
    pair_token = lax.iota(jnp.int32, pairs) // fanout
    pick = tokens - jnp.sum(jnp.where(hit, tokens - pair_token[None, :], 0), axis=1)
    sent_prob = probs.astype(BF16).astype(F32).reshape(1, pairs)
    prob = jnp.sum(jnp.where(hit, sent_prob, 0.0), axis=1).reshape(slots, n_exp, CAP)
    q_send = jnp.pad(
        prob.transpose(1, 0, 2).reshape(n_exp, 1, slots * CAP),
        ((0, 0), (0, 0), (0, LANES - slots * CAP)),
    )

    send = pl.pallas_call(
        dispatch_kernel,
        out_shape=jax.ShapeDtypeStruct((slots, n_exp, 2 * CAP, slabs, LANES), BF16),
        in_specs=[
            pl.BlockSpec(memory_space=pltpu.SMEM),
            pl.BlockSpec(memory_space=pltpu.VMEM),
            pl.BlockSpec(memory_space=pltpu.VMEM),
        ],
        out_specs=pl.BlockSpec(memory_space=pltpu.VMEM),
        scratch_shapes=[pltpu.VMEM(((tokens + 1) * slabs, LANES), F32)],
        compiler_params=pltpu.CompilerParams(vmem_limit_bytes=40 * 1024 * 1024),
    )(pick, layer_inputs, output_adjoint)

    weights = jnp.concatenate(
        [gating_kernel, expansion_kernel, contraction_kernel], axis=2
    ).transpose(1, 0, 2)
    device = jnp.where(kept, owner, -1).reshape(tokens, fanout)
    lane = (local * CAP + arrival).reshape(tokens, fanout)
    back, dw, logit_grad, router = exchange(
        n_dp,
        n_exp,
        send,
        q_send,
        weights,
        layer_inputs,
        token_experts,
        device,
        lane,
        probs,
    )
    token_grad = pl.pallas_call(
        combine_kernel,
        out_shape=jax.ShapeDtypeStruct((tokens, width), BF16),
        in_specs=[
            pl.BlockSpec(memory_space=pltpu.SMEM),
            pl.BlockSpec(memory_space=pltpu.VMEM),
            pl.BlockSpec(memory_space=pltpu.VMEM),
            pl.BlockSpec(memory_space=pltpu.VMEM),
        ],
        out_specs=pl.BlockSpec(memory_space=pltpu.VMEM),
        scratch_shapes=[pltpu.VMEM((tokens * slabs, LANES), F32)],
        compiler_params=pltpu.CompilerParams(vmem_limit_bytes=40 * 1024 * 1024),
    )(position, back, logit_grad, dispatcher_projection)

    dw = dw.transpose(1, 0, 2)
    gate_grad = dw[:, :, :hidden]
    up_grad = dw[:, :, hidden : 2 * hidden]
    down_grad = dw[:, :, 2 * hidden :]
    share = width // n_dp
    router_grad = lax.dynamic_slice(
        router.reshape(width), (lax.axis_index("dp") * share,), (share,)
    )[:, None]
    return (token_grad, gate_grad, up_grad, down_grad, router_grad)


def solution(mesh):
    return jax.shard_map(
        functools.partial(shards, mesh.shape["dp"], mesh.shape["expert"]),
        mesh=mesh,
        in_specs=(
            P(("dp", "expert"), None),
            P(("dp", "expert"), None),
            P(),
            P("dp", "expert", None),
            P("dp", "expert", None),
            P("dp", "expert", None),
            P(("dp", "expert"), None),
            P(("dp", "expert"), None),
            P(),
            P(),
        ),
        out_specs=(
            P(("dp", "expert"), None),
            P("dp", "expert", None),
            P("dp", "expert", None),
            P("dp", "expert", None),
            P("dp", "expert"),
        ),
        check_vma=False,
    )
```

profile of v0, /device:TPU:1, one launch (start us, length us, event | category | flops | bytes accessed | tf_op | source)
XLA Modules:
  0.0 244.0 jit_solution(1506340740250957950)
XLA Ops:
  0.7 0.8 multiply_add_fusion
  1.5 0.1 copy.57
  1.7 0.8 copy.58
  2.4 0.1 broadcast_in_dim.70
  2.5 0.4 select_reduce_fusion.2
  2.9 0.1 copy.59
  3.0 0.2 fusion.2
  3.3 0.1 copy.60
  3.4 0.5 select_reduce_fusion.3
  3.9 0.3 select_reduce_fusion.1
  4.4 3.8 %shard_map.137.send = bf16[2,64,10,16,128]{4,3,2,1,0:T(8,128)(2,1)S(1)} custom-call(s32[640]{0:T(1024)S(1)} %broadcast_subtract_fusion.pick, bf16[128,2048]{1,0:T(8,128)(2,1)S(1)} %copy-done.1, bf16[128,2048]{1,0:T(8,128)(2,1)S(1)} %copy-done.3), custom_call_target="tpu_custom_call" | custom-call | tf_op jit(solution)/shard_map/pallas_call | solution.py:534
  8.1 2.3 copy-done
  10.4 0.3 fusion.25
  10.8 0.1 copy.61
  10.9 0.7 convert_convert_fusion
  11.8 0.3 select_reduce_fusion
  12.1 0.2 reshape.129
  12.5 0.6 pad.4.q_send
  13.4 0.7 fusion.7
  14.1 0.1 copy.64
  14.2 0.1 copy.65
  14.4 0.1 copy.66
  14.5 1.6 maximum_bitcast_fusion.w
  16.1 0.7 copy.67.te
  16.8 211.8 %shard_map.138 = (bf16[641,16,128]{2,1,0:T(8,128)(2,1)}, f32[2,512,1152]{2,1,0:T(8,128)}, bf16[128,64]{1,0:T(8,128)(2,1)}, f32[16,128]{1,0:T(8,128)}) custom-call(bf16[2,64,10,16,128]{4,3,2,1,0:T(8,128)(2,1)} %copy-done, f32[64,1,128]{2,1,0:T(1,128)} %pad.4.q_send, bf16[2,512,1152]{2,1,0:T(8,128)(2,1)} %maximum_bitcast_fusion.w, bf16[128,2048]{1,0:T(8,128)(2,1)} %x.3, ...), custom_call_target="tpu_custom_call" | custom-call | tf_op jit(solution)/shard_map/pallas_call | solution.py:426
  228.7 2.7 %fusion.24 = (f32[512,2,384]{2,0,1:T(8,128)S(1)}, f32[512,2,384]{2,0,1:T(8,128)S(1)}, f32[512,2,384]{2,0,1:T(8,128)S(1)}) fusion(f32[512,2,1152]{2,0,1:T(8,128)} %bitcast.21), kind=kLoop, calls=%fused_computation.59 | loop fusion | bytes 9437184 | tf_op jit(solution)/shard_map/slice | solution.py:581
  231.3 2.4 copy.69
  233.7 2.4 copy.70
  236.1 2.4 copy.71
  238.4 0.3 copy.68.proj_ref
  238.7 4.0 %shard_map.139 = bf16[128,2048]{1,0:T(8,128)(2,1)} custom-call(s32[1024]{0:T(1024)S(1)} %get-tuple-element.44.place, bf16[641,16,128]{2,1,0:T(8,128)(2,1)S(1)} %copy-done.2, bf16[128,64]{1,0:T(8,128)(2,1)S(1)} %copy-done.4, bf16[2048,64]{1,0:T(8,128)(2,1)S(1)} %copy.68.proj_ref), custom_call_target="tpu_custom_call" | custom-call | tf_op jit(solution)/shard_map/pallas_call | solution.py:564
  242.7 1.3 dynamic_slice.3
  (38 shorter events, 0.8 us)
Async XLA Ops:
  0.6 2.8 %copy-start.10 = (s32[128]{0:T(128)S(1)}, s32[128]{0:T(128)}, u32[]{:S(2)}) copy-start(s32[128]{0:T(128)} %param.19) | copy-start | bytes 1540
  0.6 3.7 %copy-start.1 = (bf16[128,2048]{1,0:T(8,128)(2,1)S(1)}, bf16[128,2048]{1,0:T(8,128)(2,1)}, u32[]{:S(2)}) copy-start(bf16[128,2048]{1,0:T(8,128)(2,1)} %x.3) | copy-start | bytes 1572868
  0.7 3.7 %copy-start.3 = (bf16[128,2048]{1,0:T(8,128)(2,1)S(1)}, bf16[128,2048]{1,0:T(8,128)(2,1)}, u32[]{:S(2)}) copy-start(bf16[128,2048]{1,0:T(8,128)(2,1)} %g_ref.1) | copy-start | bytes 1572868
  4.3 6.1 %copy-start.5 = (bf16[2048,64]{0,1:T(8,128)(2,1)S(1)}, bf16[2048,64]{0,1:T(8,128)(2,1)}, u32[]{:S(2)}) copy-start(bf16[2048,64]{0,1:T(8,128)(2,1)} %param.12) | copy-start | bytes 786436
  4.3 6.4 %copy-start.9 = (s32[128,8]{0,1:T(8,128)S(1)}, s32[128,8]{0,1:T(8,128)}, u32[]{:S(2)}) copy-start(s32[128,8]{0,1:T(8,128)} %param.16) | copy-start | bytes 12292
  4.3 9.8 %copy-start.6 = (bf16[512,2,384]{2,1,0:T(2,128)(2,1)S(1)}, bf16[512,2,384]{2,1,0:T(2,128)(2,1)}, u32[]{:S(2)}) copy-start(bf16[512,2,384]{2,1,0:T(2,128)(2,1)} %param.13) | copy-start | bytes 2359300
  8.1 2.3 copy-start
  10.4 3.8 %copy-start.7 = (bf16[512,2,384]{2,1,0:T(2,128)(2,1)S(1)}, bf16[512,2,384]{2,1,0:T(2,128)(2,1)}, u32[]{:S(2)}) copy-start(bf16[512,2,384]{2,1,0:T(2,128)(2,1)} %param.14) | copy-start | bytes 2359300
  10.7 3.6 %copy-start.8 = (bf16[512,2,384]{2,1,0:T(2,128)(2,1)S(1)}, bf16[512,2,384]{2,1,0:T(2,128)(2,1)}, u32[]{:S(2)}) copy-start(bf16[512,2,384]{2,1,0:T(2,128)(2,1)} %param.15) | copy-start | bytes 2359300
  236.0 2.7 %copy-start.2 = (bf16[641,16,128]{2,1,0:T(8,128)(2,1)S(1)}, bf16[641,16,128]{2,1,0:T(8,128)(2,1)}, u32[]{:S(2)}) copy-start(bf16[641,16,128]{2,1,0:T(8,128)(2,1)} %get-tuple-element.9.back_ref) | copy-start | bytes 7876612
  236.0 2.7 %copy-start.4 = (bf16[128,64]{1,0:T(8,128)(2,1)S(1)}, bf16[128,64]{1,0:T(8,128)(2,1)}, u32[]{:S(2)}) copy-start(bf16[128,64]{1,0:T(8,128)(2,1)} %get-tuple-element.10.lg_ref) | copy-start | bytes 49156
where the time goes:
time: 244 us
  Pallas kernels  220 us (90%)
  local copies, waits for them, and re-layouts  17.5 us (7%)
  other arithmetic  5.79 us (2%)
    pallas_call x1, Pallas kernels, exchange(): pl.pallas_call(functools.partial(exchange_kernel, n_dp, n_exp), out_shape...  212 us
    unnamed x31, local copies, waits for them, and re-layouts  11.5 us

commit v1 on v0

--- a/solution.py
+++ b/solution.py
@@ -8,31 +8,23 @@
 from jax.sharding import PartitionSpec as P
 
 CAP = 5
+PLANE = 8
 LANES = 128
 MESH = pl.DeviceIdType.MESH
 F32 = jnp.float32
 BF16 = jnp.bfloat16
 
 
-def dispatch_kernel(pick, x_ref, g_ref, out_ref, flat):
+def slab_kernel(x_ref, g_ref, out_ref, flat):
     tokens, width = x_ref.shape
     slabs = width // LANES
-    slots, devs, depth = out_ref.shape[:3]
-    cap = depth // 2
-    flat[pl.ds(tokens * slabs, slabs), :] = jnp.zeros((slabs, LANES), F32)
     for which, ref in enumerate((x_ref, g_ref)):
         for a in range(slabs):
             flat[pl.ds(a, tokens, stride=slabs), :] = ref[:, a * LANES : (a + 1) * LANES].astype(F32)
-
-        def one(d, carry, which=which):
-            for s in range(slots):
-                for c in range(cap):
-                    token = pick[(s * devs + d) * cap + c]
-                    row = pl.multiple_of(token * slabs, slabs)
-                    out_ref[s, d, which * cap + c] = flat[pl.ds(row, slabs), :].astype(BF16)
-            return carry
-
-        lax.fori_loop(0, devs, one, 0)
+        out_ref[which * tokens : (which + 1) * tokens] = (
+            flat[...].astype(BF16).reshape(tokens, slabs, LANES)
+        )
+    out_ref[2 * tokens] = jnp.zeros((slabs, LANES), BF16)
 
 
 def combine_kernel(place, back_ref, lg_ref, proj_ref, out_ref, flat):
@@ -59,7 +51,8 @@
 def exchange_kernel(
     n_dp,
     n_exp,
-    send,
+    block,
+    table,
     q_send,
     w,
     x,
@@ -72,6 +65,9 @@
     lg_out,
     rcol,
     recv,
+    sb,
+    table_recv,
+    table_smem,
     q_recv,
     wf,
     flat,
@@ -82,13 +78,16 @@
     dwp,
     rs1,
     rs2,
-    dxs,
     zero,
     pg,
     pg_recv,
     rt,
     rt_recv,
     r2,
+    ring_ss,
+    ring_rs,
+    table_ss,
+    table_rs,
     tok_ss,
     tok_rs,
     q_ss,
@@ -106,20 +105,25 @@
     r2_ss,
     r2_rs,
     own_sem,
+    *blocks,
 ):
     me = lax.axis_index("expert")
     my = lax.axis_index("dp")
     right = lax.rem(my + 1, n_dp)
     far = lax.rem(my + 2, n_dp)
     left = lax.rem(my + 3, n_dp)
-    slots, _, depth, slabs, _ = recv.shape
-    cap = depth // 2
+    n_z, plane, depth, slabs, _ = sb.shape
+    slots = w.shape[0]
+    cap = depth // (2 * slots)
     rows = cap * n_exp
+    tokens = x.shape[0]
+    z, inner = lax.div(me, plane), lax.rem(me, plane)
+    above, below = lax.rem(me + plane, n_exp), lax.rem(me + n_exp - plane, n_exp)
     quarter = wf.shape[2]
     half = quarter // 2
     ff = wf.shape[3] // 3
     per = slabs // n_dp
-    chunk = min(8, n_exp)
+    chunk = plane
     others = n_exp - 1
 
     barrier = pltpu.get_barrier_semaphore()
@@ -171,29 +175,94 @@
         wait_for(wf.at[s, far, pl.ds(0, half)], w_rs.at[s, 2])
         wait_for(wf.at[s, far, pl.ds(half, half)], w_rs.at[s, 3])
 
+    whole, x_part, g_part = pl.ds(0, 2 * tokens), pl.ds(0, tokens), pl.ds(tokens, tokens)
+    steps = n_z // 2
+    up = [block] + list(blocks[: steps - 1])
+    down = [block] + list(blocks[steps - 1 : 2 * steps - 2])
+    opposite = blocks[2 * steps - 2]
+
+    def ring(t):
+        last = t == steps - 1
+        for n, (held, other, part) in enumerate(((up, above, x_part), (down, below, g_part))):
+            part = part if last else whole
+            target = opposite if last else held[t + 1]
+            to_exp(
+                held[t].at[part], target.at[part], ring_ss.at[n, t], ring_rs.at[n, t], other
+            ).start()
+
+    def ring_wait(t):
+        last = t == steps - 1
+        for n, (held, part) in enumerate(((up, x_part), (down, g_part))):
+            target = opposite if last else held[t + 1]
+            wait_for(target.at[part if last else whole], ring_rs.at[n, t])
+
+    def share(rel, held):
+        source = lax.rem(z + rel, n_z) * plane + inner
+
+        def one(d, carry):
+            for s in range(slots):
+                for c in range(cap):
+                    token = table_smem[rel, 0, (d * slots + s) * cap + c]
+                    other = jnp.minimum(token + tokens, 2 * tokens)
+                    sb[rel, d, s * 2 * cap + c] = held[token]
+                    sb[rel, d, s * 2 * cap + cap + c] = held[other]
+            return carry
+
+        lax.fori_loop(0, plane, one, 0)
+
+        def out(i, carry):
+            d = lax.rem(inner + i, plane)
+            to_exp(sb.at[rel, d], recv.at[source], tok_ss, tok_rs, z * plane + d).start()
+            return carry
+
+        lax.fori_loop(1, plane, out, 0)
+        recv[source] = sb[rel, inner]
+
+    ring(0)
     w_first(0)
+    for rel in range(1, n_z):
+        to_exp(
+            table.at[lax.rem(z + rel, n_z)],
+            table_recv.at[n_z - rel],
+            table_ss,
+            table_rs,
+            lax.rem(me + rel * plane, n_exp),
+        ).start()
+    table_recv[0] = table[z]
     own = [pltpu.make_async_copy(w.at[s], wf.at[s, my], own_sem.at[s]) for s in range(slots)]
-    own += [
-        pltpu.make_async_copy(send.at[s, me], recv.at[s, me], own_sem.at[slots + s])
-        for s in range(slots)
-    ]
     for copy in own:
         copy.start()
-    to_all(lambda d: to_exp(send.at[0, d], recv.at[0, me], tok_ss.at[0], tok_rs.at[0], d))
     to_all(lambda d: to_exp(q_send.at[d], q_recv.at[me], q_ss, q_rs, d))
-    to_all(lambda d: to_exp(send.at[1, d], recv.at[1, me], tok_ss.at[1], tok_rs.at[1], d))
     q_recv[me] = q_send[me]
     zero[...] = jnp.zeros_like(zero)
     zero_copy = pltpu.make_async_copy(zero, back.at[slots * rows], own_sem.at[2 * slots])
     zero_copy.start()
-    w_second(0)
-    w_first(1)
+    for held in blocks:
+        held[2 * tokens] = jnp.zeros((slabs, LANES), BF16)
+    wait_for(table_recv.at[pl.ds(0, n_z - 1)], table_rs)
+    to_smem = pltpu.make_async_copy(table_recv, table_smem, own_sem.at[slots])
+    to_smem.start()
+    to_smem.wait()
+    share(0, block)
+    for t in range(steps - 1):
+        ring_wait(t)
+        ring(t + 1)
+        if t == 0:
+            w_second(0)
+            w_first(1)
+        if t == steps - 2:
+            w_second(1)
+        share(n_z - t - 1, up[t + 1])
+        share(t + 1, down[t + 1])
+    ring_wait(steps - 1)
+    share(steps, opposite)
 
     def to_matrix(s, which, out):
         def unpack(i, carry):
-            block = recv[s, pl.ds(i * chunk, chunk), which * cap : (which + 1) * cap]
+            first = (2 * s + which) * cap
+            part = recv[pl.ds(i * chunk, chunk), first : first + cap]
             size = chunk * cap * slabs
-            flat[pl.ds(pl.multiple_of(i * size, size), size), :] = block.astype(F32).reshape(
+            flat[pl.ds(pl.multiple_of(i * size, size), size), :] = part.astype(F32).reshape(
                 size, LANES
             )
             return carry
@@ -279,8 +348,10 @@
 
         def pack(i, carry):
             size = chunk * cap * slabs
-            block = flat[pl.ds(pl.multiple_of(i * size, size), size), :]
-            dxs[s, pl.ds(i * chunk, chunk)] = block.astype(BF16).reshape(chunk, cap, slabs, LANES)
+            part = flat[pl.ds(pl.multiple_of(i * size, size), size), :]
+            sb[i, :, s * cap : (s + 1) * cap] = part.astype(BF16).reshape(
+                chunk, cap, slabs, LANES
+            )
             return carry
 
         lax.fori_loop(0, n_exp // chunk, pack, 0)
@@ -288,9 +359,14 @@
     def place(s, d):
         return back.at[pl.ds((s * n_exp + d) * cap, cap)]
 
+    def dx_of(s, d):
+        return sb.at[lax.div(d, plane), lax.rem(d, plane), pl.ds(s * cap, cap)]
+
     def dx_start(s):
-        pltpu.make_async_copy(dxs.at[s, me], place(s, me), own_sem.at[2 * slots + 1 + s]).start()
-        to_all(lambda d: to_exp(dxs.at[s, d], place(s, me), dx_ss.at[s], dx_rs.at[s], d))
+        pltpu.make_async_copy(
+            dx_of(s, me), place(s, me), own_sem.at[2 * slots + 1 + s]
+        ).start()
+        to_all(lambda d: to_exp(dx_of(s, d), place(s, me), dx_ss.at[s], dx_rs.at[s], d))
 
     def sum_first(s):
         to_dp(
@@ -316,30 +392,24 @@
         wait_for(rs2.at[s, 1], g_rs.at[s, 3])
         dw[s] = dwp[s, my].astype(F32) + rs2[s, 0].astype(F32) + rs2[s, 1].astype(F32)
 
-    def tokens_here(s):
-        wait_for(recv.at[s, pl.ds(0, others)], tok_rs.at[s])
-        own[slots + s].wait()
-
-    tokens_here(0)
+    wait_for(recv.at[pl.ds(0, n_z * (plane - 1))], tok_rs)
     wait_for(q_recv.at[pl.ds(0, others)], q_rs)
     own[0].wait()
     w_end(0)
-    table = forward(0)
+    grads = forward(0)
     weight_grad(0, far)
     sum_first(0)
-    w_second(1)
     weight_grad(0, right)
     weight_grad(0, left)
     weight_grad(0, my)
+    wait_for(recv.at[pl.ds(0, n_z * (plane - 1))], tok_ss)
     input_grad(0)
-    sum_second(0)
+    dx_start(0)
     own[1].wait()
     w_end(1)
-
-    tokens_here(1)
-    dx_start(0)
-    table = table + forward(1)
-    pg[...] = table.reshape(pg.shape)
+    sum_second(0)
+    grads = grads + forward(1)
+    pg[...] = grads.reshape(pg.shape)
     to_all(lambda d: to_exp(pg.at[d], pg_recv.at[me], pg_ss, pg_rs, d))
     pg_recv[me] = pg[me]
     weight_grad(1, far)
@@ -353,7 +423,7 @@
 
     wait_for(pg_recv.at[pl.ds(0, others)], pg_rs)
     grads = pg_recv[...].reshape(n_exp, LANES).astype(BF16)
-    tokens, fanout = te.shape
+    fanout = te.shape[1]
     dev_ids = lax.broadcasted_iota(jnp.int32, (tokens, n_exp), 1)
     lane_ids = lax.broadcasted_iota(jnp.int32, (tokens, LANES), 1)
     pair = []
@@ -398,8 +468,11 @@
     wait_for(rt.at[pl.ds(0, others)], rt_ss)
     for n in range(n_dp - 1):
         wait_for(r2.at[0], r2_ss.at[n])
+    wait_for(table.at[pl.ds(0, n_z - 1)], table_ss)
+    for n, part in enumerate((x_part, g_part)):
+        for t in range(steps):
+            wait_for(block.at[part if t == steps - 1 else whole], ring_ss.at[n, t])
     for s in range(slots):
-        wait_for(recv.at[s, pl.ds(0, others)], tok_ss.at[s])
         wait_for(wf.at[s, 0], w_ss.at[s, 0])
         wait_for(wf.at[s, 0], w_ss.at[s, 1])
         for n in (2, 3):
@@ -407,14 +480,19 @@
         for n in (0, 1):
             wait_for(rs1.at[s, n], g_ss.at[s, n])
             wait_for(rs2.at[s, n], g_ss.at[s, 2 + n])
-        pltpu.make_async_copy(dxs.at[s, me], place(s, me), own_sem.at[2 * slots + 1 + s]).wait()
-        wait_for(dxs.at[s, pl.ds(0, others)], dx_ss.at[s])
-        wait_for(dxs.at[s, pl.ds(0, others)], dx_rs.at[s])
-
-
-def exchange(n_dp, n_exp, send, q_send, w, x, te, dev, lane, probs):
-    slots, _, depth, slabs, _ = send.shape
-    cap = depth // 2
+        pltpu.make_async_copy(
+            dx_of(s, me), place(s, me), own_sem.at[2 * slots + 1 + s]
+        ).wait()
+        wait_for(back.at[pl.ds(0, others * cap)], dx_ss.at[s])
+        wait_for(back.at[pl.ds(0, others * cap)], dx_rs.at[s])
+
+
+def exchange(n_dp, n_exp, block, table, q_send, w, x, te, dev, lane, probs):
+    slots = w.shape[0]
+    cap = CAP
+    slabs = block.shape[1]
+    n_z = table.shape[0]
+    plane = n_exp // n_z
     rows = cap * n_exp
     quarter, wide = w.shape[1:]
     half = quarter // 2
@@ -431,10 +509,13 @@
             jax.ShapeDtypeStruct((tokens, n_exp), BF16),
             jax.ShapeDtypeStruct((slabs, LANES), F32),
         ),
-        in_specs=[hbm, vmem, hbm, vmem, vmem, vmem, vmem, vmem],
+        in_specs=[vmem, vmem, vmem, hbm, vmem, vmem, vmem, vmem, vmem],
         out_specs=(hbm, vmem, vmem, vmem),
         scratch_shapes=[
-            pltpu.VMEM(send.shape, BF16),
+            pltpu.VMEM((n_exp, 2 * slots * cap, slabs, LANES), BF16),
+            pltpu.VMEM((n_z, plane, 2 * slots * cap, slabs, LANES), BF16),
+            pltpu.VMEM((n_z, 1, LANES), jnp.int32),
+            pltpu.SMEM((n_z, 1, LANES), jnp.int32),
             pltpu.VMEM((n_exp, 1, LANES), F32),
             pltpu.VMEM((slots, n_dp, quarter, wide), BF16),
             pltpu.VMEM((rows * slabs, LANES), F32),
@@ -445,15 +526,18 @@
             pltpu.VMEM((slots, n_dp, quarter, wide), BF16),
             pltpu.VMEM((slots, 2, half, wide), BF16),
             pltpu.VMEM((slots, 2, quarter, wide), BF16),
-            pltpu.VMEM((slots, n_exp, cap, slabs, LANES), BF16),
             pltpu.VMEM((slabs, LANES), BF16),
             pltpu.VMEM((n_exp, 1, LANES), F32),
             pltpu.VMEM((n_exp, 1, LANES), F32),
             pltpu.VMEM((n_exp, slabs, LANES), BF16),
             pltpu.VMEM((n_exp, slabs, LANES), BF16),
             pltpu.VMEM((n_dp, slabs, LANES), F32),
-            dma((slots,)),
-            dma((slots,)),
+            dma((2, n_z // 2)),
+            dma((2, n_z // 2)),
+            dma,
+            dma,
+            dma,
+            dma,
             dma,
             dma,
             dma((slots, 4)),
@@ -469,11 +553,12 @@
             dma((n_dp - 1,)),
             dma((n_dp - 1,)),
             dma((3 * slots + 1,)),
-        ],
+        ]
+        + [pltpu.VMEM(block.shape, BF16)] * (n_z - 1),
         compiler_params=pltpu.CompilerParams(
             collective_id=0, has_side_effects=True, vmem_limit_bytes=60 * 1024 * 1024
         ),
-    )(send, q_send, w, x, te, dev, lane, probs)
+    )(block, table, q_send, w, x, te, dev, lane, probs)
 
 
 def shards(
@@ -523,7 +608,7 @@
     position = jnp.where(kept, (local * n_exp + owner) * CAP + arrival, sent)
     hit = position[None, :] == lax.iota(jnp.int32, sent)[:, None]
     pair_token = lax.iota(jnp.int32, pairs) // fanout
-    pick = tokens - jnp.sum(jnp.where(hit, tokens - pair_token[None, :], 0), axis=1)
+    pick = 2 * tokens - jnp.sum(jnp.where(hit, 2 * tokens - pair_token[None, :], 0), axis=1)
     sent_prob = probs.astype(BF16).astype(F32).reshape(1, pairs)
     prob = jnp.sum(jnp.where(hit, sent_prob, 0.0), axis=1).reshape(slots, n_exp, CAP)
     q_send = jnp.pad(
@@ -531,18 +616,19 @@
         ((0, 0), (0, 0), (0, LANES - slots * CAP)),
     )
 
-    send = pl.pallas_call(
-        dispatch_kernel,
-        out_shape=jax.ShapeDtypeStruct((slots, n_exp, 2 * CAP, slabs, LANES), BF16),
-        in_specs=[
-            pl.BlockSpec(memory_space=pltpu.SMEM),
-            pl.BlockSpec(memory_space=pltpu.VMEM),
-            pl.BlockSpec(memory_space=pltpu.VMEM),
-        ],
+    n_z = n_exp // PLANE
+    table = jnp.pad(
+        pick.reshape(slots, n_z, PLANE, CAP).transpose(1, 2, 0, 3).reshape(n_z, 1, slots * PLANE * CAP),
+        ((0, 0), (0, 0), (0, LANES - slots * PLANE * CAP)),
+    )
+    block = pl.pallas_call(
+        slab_kernel,
+        out_shape=jax.ShapeDtypeStruct((2 * tokens + 1, slabs, LANES), BF16),
+        in_specs=[pl.BlockSpec(memory_space=pltpu.VMEM)] * 2,
         out_specs=pl.BlockSpec(memory_space=pltpu.VMEM),
-        scratch_shapes=[pltpu.VMEM(((tokens + 1) * slabs, LANES), F32)],
+        scratch_shapes=[pltpu.VMEM((tokens * slabs, LANES), F32)],
         compiler_params=pltpu.CompilerParams(vmem_limit_bytes=40 * 1024 * 1024),
-    )(pick, layer_inputs, output_adjoint)
+    )(layer_inputs, output_adjoint)
 
     weights = jnp.concatenate(
         [gating_kernel, expansion_kernel, contraction_kernel], axis=2
@@ -552,7 +638,8 @@
     back, dw, logit_grad, router = exchange(
         n_dp,
         n_exp,
-        send,
+        block,
+        table,
         q_send,
         weights,
         layer_inputs,

time: 244 us -> 234 us (0.959)
  Pallas kernels: 220 us -> 207 us
    pallas_call x1, Pallas kernels: 212 us -> 202 us  [exchange(): pl.pallas_call(functools.partial(exchange_kernel, n_dp, n_exp), out_shape...]
    pallas_call x1, Pallas kernels: 3.75 us -> 1.15 us  [shards(): pl.pallas_call(slab_kernel, out_shape=jax.ShapeDtypeStruct((2 * tokens +...]
where the time goes in v1:
time: 234 us
  Pallas kernels  207 us (88%)
  local copies, waits for them, and re-layouts  19.7 us (8%)
  other arithmetic  5.77 us (2%)
    pallas_call x1, Pallas kernels, exchange(): pl.pallas_call(functools.partial(exchange_kernel, n_dp, n_exp), out_shape...  202 us
    unnamed x31, local copies, waits for them, and re-layouts  12.8 us

profile of v1, /device:TPU:1, one launch (start us, length us, event | category | flops | bytes accessed | tf_op | source)
XLA Modules:
  0.0 233.9 jit_solution(14363634499113908514)
XLA Ops:
  0.7 0.9 copy.62
  1.5 0.1 broadcast_in_dim.70
  1.6 0.7 multiply_add_fusion
  2.3 0.1 copy.61
  2.5 0.4 select_reduce_fusion.2
  3.0 0.2 fusion.2
  3.3 0.1 copy.64
  3.5 0.5 select_reduce_fusion.3
  4.0 1.1 shard_map.137.block
  5.2 1.0 copy-done.1
  6.2 0.3 select_reduce_fusion.1
  6.5 0.2 sub.56
  6.8 0.1 reshape.136
  6.9 0.6 pad.8.table
  7.5 0.3 fusion.25
  8.0 0.7 convert_convert_fusion
  8.8 0.3 select_reduce_fusion
  9.2 0.2 reshape.137
  9.5 0.6 pad.9.q_send
  10.5 1.7 maximum_bitcast_fusion.w
  12.2 0.7 copy.73.te
  13.2 0.7 fusion.7
  13.9 202.1 %shard_map.138 = (bf16[641,16,128]{2,1,0:T(8,128)(2,1)}, f32[2,512,1152]{2,1,0:T(8,128)}, bf16[128,64]{1,0:T(8,128)(2,1)}, f32[16,128]{1,0:T(8,128)}) custom-call(bf16[257,16,128]{2,1,0:T(8,128)(2,1)} %copy-done.1, s32[8,1,128]{2,1,0:T(1,128)} %pad.8.table, f32[64,1,128]{2,1,0:T(1,128)} %pad.9.q_send, bf16[2,512,1152]{2,1,0:T(8,128)(2,1)} %maximum_bitcast_fusion.w, ...), custom_call_target="tpu_custom_call" | custom-call | tf_op jit(solution)/shard_map/pallas_call | solution.py:504
  216.0 0.3 copy.74.proj_ref
  216.3 1.7 copy-done.2
  218.1 0.8 copy-done.4
  218.8 4.0 %shard_map.139 = bf16[128,2048]{1,0:T(8,128)(2,1)} custom-call(s32[1024]{0:T(1024)S(1)} %get-tuple-element.44.place, bf16[641,16,128]{2,1,0:T(8,128)(2,1)S(1)} %copy-done.2, bf16[128,64]{1,0:T(8,128)(2,1)S(1)} %copy-done.4, bf16[2048,64]{1,0:T(8,128)(2,1)S(1)} %copy.74.proj_ref), custom_call_target="tpu_custom_call" | custom-call | tf_op jit(solution)/shard_map/pallas_call | solution.py:651
  222.8 2.7 %fusion.24 = (f32[512,2,384]{2,0,1:T(8,128)S(1)}, f32[512,2,384]{2,0,1:T(8,128)S(1)}, f32[512,2,384]{2,0,1:T(8,128)S(1)}) fusion(f32[512,2,1152]{2,0,1:T(8,128)} %bitcast.23), kind=kLoop, calls=%fused_computation.59 | loop fusion | bytes 9437184 | tf_op jit(solution)/shard_map/slice | solution.py:668
  225.5 2.4 %copy.75 = f32[512,2,384]{2,1,0:T(2,128)} copy(f32[512,2,384]{2,0,1:T(8,128)S(1)} %get-tuple-element.41) | data formatting | bytes 3145728
  227.9 2.4 %copy.76 = f32[512,2,384]{2,1,0:T(2,128)} copy(f32[512,2,384]{2,0,1:T(8,128)S(1)} %get-tuple-element.40) | data formatting | bytes 3145728
  230.2 2.4 %copy.77 = f32[512,2,384]{2,1,0:T(2,128)} copy(f32[512,2,384]{2,0,1:T(8,128)S(1)} %get-tuple-element.39) | data formatting | bytes 3145728
  232.6 1.3 dynamic_slice.3
  (42 shorter events, 1.4 us)
Async XLA Ops:
  0.6 2.8 %copy-start.10 = (s32[128]{0:T(128)S(1)}, s32[128]{0:T(128)}, u32[]{:S(2)}) copy-start(s32[128]{0:T(128)} %param.19) | copy-start | bytes 1540
  0.6 3.3 %copy-start = (bf16[128,2048]{1,0:T(8,128)(2,1)S(1)}, bf16[128,2048]{1,0:T(8,128)(2,1)}, u32[]{:S(2)}) copy-start(bf16[128,2048]{1,0:T(8,128)(2,1)} %x.5) | copy-start | bytes 1572868
  0.7 3.3 %copy-start.3 = (bf16[128,2048]{1,0:T(8,128)(2,1)S(1)}, bf16[128,2048]{1,0:T(8,128)(2,1)}, u32[]{:S(2)}) copy-start(bf16[128,2048]{1,0:T(8,128)(2,1)} %g_ref.1) | copy-start | bytes 1572868
  3.2 4.3 %copy-start.5 = (bf16[2048,64]{0,1:T(8,128)(2,1)S(1)}, bf16[2048,64]{0,1:T(8,128)(2,1)}, u32[]{:S(2)}) copy-start(bf16[2048,64]{0,1:T(8,128)(2,1)} %param.12) | copy-start | bytes 786436
  3.3 4.5 %copy-start.9 = (s32[128,8]{0,1:T(8,128)S(1)}, s32[128,8]{0,1:T(8,128)}, u32[]{:S(2)}) copy-start(s32[128,8]{0,1:T(8,128)} %param.16) | copy-start | bytes 12292
  3.3 6.9 %copy-start.6 = (bf16[512,2,384]{2,1,0:T(2,128)(2,1)S(1)}, bf16[512,2,384]{2,1,0:T(2,128)(2,1)}, u32[]{:S(2)}) copy-start(bf16[512,2,384]{2,1,0:T(2,128)(2,1)} %param.15) | copy-start | bytes 2359300
  4.0 6.3 %copy-start.7 = (bf16[512,2,384]{2,1,0:T(2,128)(2,1)S(1)}, bf16[512,2,384]{2,1,0:T(2,128)(2,1)}, u32[]{:S(2)}) copy-start(bf16[512,2,384]{2,1,0:T(2,128)(2,1)} %param.14) | copy-start | bytes 2359300
  5.2 1.0 copy-start.1
  6.1 4.3 %copy-start.8 = (bf16[512,2,384]{2,1,0:T(2,128)(2,1)S(1)}, bf16[512,2,384]{2,1,0:T(2,128)(2,1)}, u32[]{:S(2)}) copy-start(bf16[512,2,384]{2,1,0:T(2,128)(2,1)} %param.13) | copy-start | bytes 2359300
  216.3 1.7 copy-start.2
  218.1 0.8 copy-start.4

commit v2 on v1

v2 whole, which is shorter than its diff:
```python
import functools

import jax
import jax.numpy as jnp
from jax import lax
from jax.experimental import pallas as pl
from jax.experimental.pallas import tpu as pltpu
from jax.sharding import PartitionSpec as P

CAP = 5
PLANE = 8
LANES = 128
MESH = pl.DeviceIdType.MESH
F32 = jnp.float32
BF16 = jnp.bfloat16


def slab_kernel(x_ref, g_ref, out_ref, flat):
    tokens, width = x_ref.shape
    slabs = width // LANES
    for which, ref in enumerate((x_ref, g_ref)):
        for a in range(slabs):
            flat[pl.ds(a, tokens, stride=slabs), :] = ref[:, a * LANES : (a + 1) * LANES].astype(F32)
        out_ref[which * tokens : (which + 1) * tokens] = (
            flat[...].astype(BF16).reshape(tokens, slabs, LANES)
        )
    out_ref[2 * tokens] = jnp.zeros((slabs, LANES), BF16)


def exchange_kernel(
    n_dp,
    n_exp,
    place,
    block,
    table,
    q_table,
    w,
    x,
    proj,
    te,
    dev,
    lane,
    probs,
    token_grad,
    dw,
    rcol,
    recv,
    sb,
    dxs,
    back,
    table_recv,
    table_smem,
    q_mid,
    q_all,
    wf,
    flat,
    xm,
    gm,
    gu,
    act_s,
    q_col,
    dwp,
    from_mate,
    from_mate2,
    from_partner,
    pg,
    pg_recv,
    rt,
    rt_recv,
    r2,
    sums,
    ring_ss,
    ring_rs,
    table_ss,
    table_rs,
    qt_ss,
    qt_rs,
    q_ss,
    q_rs,
    tok_ss,
    tok_rs,
    w_ss,
    w_rs,
    g_ss,
    g_rs,
    dx_ss,
    dx_rs,
    pg_ss,
    pg_rs,
    rt_ss,
    rt_rs,
    r2_ss,
    r2_rs,
    own_sem,
    *blocks,
):
    me = lax.axis_index("expert")
    my = lax.axis_index("dp")
    partner = n_dp - 1 - my
    slot = lax.div(my, 2)
    other_slot = 1 - slot
    mate = my + 1 - 2 * lax.rem(my, 2)
    corner = n_dp - 1 - mate
    n_z, sides, depth, slabs, _ = sb.shape
    plane = sides // 2
    cap = depth // 2
    group = sides * cap
    rows = n_z * group
    tokens = x.shape[0]
    z, inner = lax.div(me, plane), lax.rem(me, plane)
    above, below = lax.rem(me + plane, n_exp), lax.rem(me + n_exp - plane, n_exp)
    quarter = wf.shape[1]
    half = quarter // 2
    ff = wf.shape[2] // 3
    per = slabs // n_dp
    others = n_exp - 1

    barrier = pltpu.get_barrier_semaphore()

    def greet(d, e):
        pl.semaphore_signal(
            barrier, inc=1, device_id={"dp": d, "expert": e}, device_id_type=MESH
        )

    def greet_both(i, carry):
        greet(my, lax.rem(me + i, n_exp))
        greet(partner, lax.rem(me + i, n_exp))
        return carry

    greet(mate, me)
    greet(corner, me)
    greet(partner, me)
    lax.fori_loop(1, n_exp, greet_both, 0)
    pl.semaphore_wait(barrier, 2 * n_exp + 1)

    def to(src, dst, ss, rs, d, e):
        return pltpu.make_async_remote_copy(
            src, dst, ss, rs, device_id={"dp": d, "expert": e}, device_id_type=MESH
        )

    def wait_for(ref, sem):
        pltpu.make_async_copy(ref, ref, sem).wait()

    whole, x_part, g_part = pl.ds(0, 2 * tokens), pl.ds(0, tokens), pl.ds(tokens, tokens)
    steps = n_z // 2
    up = [block] + list(blocks[: steps - 1])
    down = [block] + list(blocks[steps - 1 : 2 * steps - 2])
    opposite = blocks[2 * steps - 2]

    def ring(t):
        last = t == steps - 1
        for n, (held, e, part) in enumerate(((up, above, x_part), (down, below, g_part))):
            part = part if last else whole
            target = opposite if last else held[t + 1]
            to(
                held[t].at[part], target.at[part], ring_ss.at[n, t], ring_rs.at[n, t], my, e
            ).start()

    def ring_wait(t):
        last = t == steps - 1
        for n, (held, part) in enumerate(((up, x_part), (down, g_part))):
            target = opposite if last else held[t + 1]
            wait_for(target.at[part if last else whole], ring_rs.at[n, t])

    def share(rel, held):
        def one(d, carry):
            for side, s in enumerate((slot, other_slot)):
                first = (2 * d + s) * cap
                for c in range(cap):
                    token = table_smem[rel, 0, first + c]
                    sb[rel, side * plane + d, c] = held[token]
                    sb[rel, side * plane + d, cap + c] = held[
                        jnp.minimum(token + tokens, 2 * tokens)
                    ]
            return carry

        lax.fori_loop(0, plane, one, 0)

        def out(i, carry):
            d = lax.rem(inner + i, plane)
            for side, y in enumerate((my, partner)):
                to(
                    sb.at[rel, side * plane + d],
                    recv.at[rel, side * plane + inner],
                    tok_ss,
                    tok_rs.at[rel],
                    y,
                    z * plane + d,
                ).start()
            return carry

        to(
            sb.at[rel, plane + inner],
            recv.at[rel, plane + inner],
            tok_ss,
            tok_rs.at[rel],
            partner,
            me,
        ).start()
        lax.fori_loop(1, plane, out, 0)
        recv[rel, inner] = sb[rel, inner]

    ring(0)
    to(w.at[slot], wf.at[my], w_ss.at[0], w_rs.at[0], mate, me).start()
    to(w.at[other_slot], wf.at[my], w_ss.at[1], w_rs.at[1], partner, me).start()
    own_w = pltpu.make_async_copy(w.at[slot], wf.at[my], own_sem.at[0])
    own_w.start()
    for source, target, ss, rs in (
        (table, table_recv, table_ss, table_rs),
        (q_table, q_mid, qt_ss, qt_rs),
    ):
        for rel in range(1, n_z):
            to(
                source.at[lax.rem(z + rel, n_z)],
                target.at[n_z - rel],
                ss,
                rs,
                my,
                lax.rem(me + rel * plane, n_exp),
            ).start()
        target[0] = source[z]
    for held in blocks:
        held[2 * tokens] = jnp.zeros((slabs, LANES), BF16)
    back[2 * n_exp * cap] = jnp.zeros((slabs, LANES), BF16)
    wait_for(table_recv.at[pl.ds(0, n_z - 1)], table_rs)
    to_smem = pltpu.make_async_copy(table_recv, table_smem, own_sem.at[1])
    to_smem.start()
    wait_for(q_mid.at[pl.ds(0, n_z - 1)], qt_rs)

    def q_out(i, carry):
        e = z * plane + lax.rem(inner + i, plane)
        for side, y in enumerate((my, partner)):
            to(q_mid, q_all.at[side * plane + inner], q_ss, q_rs, y, e).start()
        return carry

    to(q_mid, q_all.at[plane + inner], q_ss, q_rs, partner, me).start()
    lax.fori_loop(1, plane, q_out, 0)
    q_all[inner] = q_mid[...]
    to_smem.wait()

    lanes = lax.broadcasted_iota(jnp.int32, (sides, LANES), 1)

    def to_matrix(rel, which, out):
        part = recv[rel, :, which * cap : (which + 1) * cap]
        flat[...] = part.astype(F32).reshape(group * slabs, LANES)

        def gather(p, carry):
            for b in range(per):
                for c in range(cap):
                    value = flat[pl.ds(c * slabs + p * per + b, sides, stride=cap * slabs), :]
                    first = rel * group + c * sides
                    out[p, first : first + sides, b * LANES : (b + 1) * LANES] = value.astype(BF16)
            return carry

        lax.fori_loop(0, n_dp, gather, 0)

    def process(rel):
        wait_for(recv.at[rel, pl.ds(0, sides - 1)], tok_rs.at[rel])
        here = slice(rel * group, (rel + 1) * group)
        to_matrix(rel, 0, xm)
        to_matrix(rel, 1, gm)
        weights = q_all[:, rel].reshape(sides, LANES)
        weight = jnp.concatenate(
            [
                jnp.sum(
                    jnp.where(lanes == (2 * inner + slot) * cap + c, weights, 0.0),
                    axis=1,
                    keepdims=True,
                )
                for c in range(cap)
            ],
            axis=0,
        )
        q_col[here] = jnp.broadcast_to(weight, (group, LANES))

        def project(p, carry):
            gate_up, down = carry
            gate_up = gate_up + jnp.dot(
                xm[p, here], wf[p, :, : 2 * ff], preferred_element_type=F32
            )
            down = down + jnp.dot(gm[p, here], wf[p, :, 2 * ff :], preferred_element_type=F32)
            return gate_up, down

        gate_up, down = lax.fori_loop(
            0, n_dp, project, (jnp.zeros((group, 2 * ff), F32), jnp.zeros((group, ff), F32))
        )
        gate, up_value = gate_up[:, :ff], gate_up[:, ff:]
        sig = jax.nn.sigmoid(gate)
        silu = gate * sig
        act = (silu * up_value).astype(BF16)
        act_s[here] = act
        grad = jnp.sum(act.astype(F32) * down, axis=1, keepdims=True).astype(BF16).astype(F32)
        act_grad = weight * down
        gu[here, :ff] = (act_grad * up_value * sig * (1.0 + gate * (1.0 - sig))).astype(BF16)
        gu[here, ff:] = (act_grad * silu).astype(BF16)
        grads = jnp.zeros((sides, LANES), F32)
        for c in range(cap):
            grads = jnp.where(
                lanes == slot * cap + c, grad[c * sides : (c + 1) * sides], grads
            )
        pg[rel] = grads.reshape(sides, 1, LANES)

        def expand(p, carry):
            value = lax.dot_general(
                gu[here],
                wf[p, :, : 2 * ff],
                (((1,), (1,)), ((), ())),
                preferred_element_type=F32,
            )
            for b in range(per):
                for c in range(cap):
                    flat[pl.ds(c * slabs + p * per + b, sides, stride=cap * slabs), :] = value[
                        c * sides : (c + 1) * sides, b * LANES : (b + 1) * LANES
                    ]
            return carry

        lax.fori_loop(0, n_dp, expand, 0)
        dxs[rel] = flat[...].astype(BF16).reshape(sides, cap, slabs, LANES)

    def send_back(rel, source, target, ss, rs):
        first = lax.rem(z + rel, n_z) * plane

        def both(i, carry):
            d = lax.rem(inner + i, plane)
            for side, y in enumerate((my, partner)):
                to(source.at[rel, side * plane + d], target, ss, rs, y, first + d).start()
            return carry

        if rel:
            lax.fori_loop(0, plane, both, 0)
        else:
            to(source.at[rel, plane + inner], target, ss, rs, partner, me).start()
            lax.fori_loop(1, plane, both, 0)

    spot = slot * n_exp + me
    own_rows = pl.ds(spot * cap, cap)

    def pg_start(rel):
        send_back(rel, pg, pg_recv.at[spot], pg_ss, pg_rs)
        if rel == 0:
            pg_recv[spot] = pg[0, inner]

    def dx_start(rel):
        send_back(rel, dxs, back.at[own_rows], dx_ss, dx_rs)
        if rel == 0:
            back[own_rows] = dxs[0, inner]

    def weight_grad(p):
        both = (((0,), (0,)), ((), ()))
        dwp[p, :, : 2 * ff] = lax.dot_general(
            xm[p], gu[...], both, preferred_element_type=F32
        ).astype(BF16)
        out_grad = jnp.concatenate(
            [
                (q_col[...] * gm[p, :, n * LANES : (n + 1) * LANES].astype(F32)).astype(BF16)
                for n in range(quarter // LANES)
            ],
            axis=1,
        )
        dwp[p, :, 2 * ff :] = lax.dot_general(
            out_grad, act_s[...], both, preferred_element_type=F32
        ).astype(BF16)

    share(0, block)
    done = [0]
    for t in range(steps - 1):
        ring_wait(t)
        ring(t + 1)
        if t == 0:
            wait_for(wf.at[partner], w_rs.at[1])
            to(wf.at[partner], wf.at[partner], w_ss.at[2], w_rs.at[2], mate, me).start()
        share(n_z - t - 1, up[t + 1])
        share(t + 1, down[t + 1])
        if t == steps - 2:
            own_w.wait()
            wait_for(wf.at[mate], w_rs.at[0])
            wait_for(wf.at[corner], w_rs.at[2])
            wait_for(q_all.at[pl.ds(0, sides - 1)], q_rs)
            for rel in done:
                process(rel)
                pg_start(rel)
            last = (n_z - t - 1, t + 1)
        else:
            done += [n_z - t - 1, t + 1]
    ring_wait(steps - 1)
    share(steps, opposite)
    for rel in done:
        dx_start(rel)
    for rel in last:
        process(rel)
        pg_start(rel)
        dx_start(rel)
    process(steps)
    pg_start(steps)

    def give(n, source, target, d):
        to(source, target, g_ss.at[n], g_rs.at[n], d, me).start()

    weight_grad(corner)
    for n in range(2):
        part = pl.ds(n * half, half)
        give(n, dwp.at[corner, part], from_mate.at[part], mate)
    dx_start(steps)
    weight_grad(mate)
    give(2, dwp.at[mate], from_mate2, mate)
    weight_grad(partner)
    for n in range(2):
        part = pl.ds(n * half, half)
        wait_for(from_mate.at[part], g_rs.at[n])
        dwp[partner, part] = (
            dwp[partner, part].astype(F32) + from_mate[part].astype(F32)
        ).astype(BF16)
        give(3 + n, dwp.at[partner, part], from_partner.at[part], partner)
    weight_grad(my)

    wait_for(pg_recv.at[pl.ds(0, 2 * n_exp - 1)], pg_rs)
    grads = pg_recv[...].reshape(2 * n_exp, LANES)
    grads = (grads[:n_exp] + grads[n_exp:]).astype(BF16)
    fanout = te.shape[1]
    dev_ids = lax.broadcasted_iota(jnp.int32, (tokens, n_exp), 1)
    lane_ids = lax.broadcasted_iota(jnp.int32, (tokens, LANES), 1)
    pair = []
    weighted = jnp.zeros((tokens, 1), F32)
    for k in range(fanout):
        hit = (dev[:, k : k + 1] == dev_ids).astype(F32).astype(BF16)
        spread = jnp.dot(hit, grads, preferred_element_type=F32)
        value = jnp.sum(
            jnp.where(lane[:, k : k + 1] == lane_ids, spread, 0.0), axis=1, keepdims=True
        )
        pair.append(value)
        weighted = weighted + probs[:, k : k + 1] * value
    logit = jnp.zeros((tokens, n_exp), F32)
    for k in range(fanout):
        chosen = probs[:, k : k + 1] * (pair[k] - weighted)
        logit = logit + jnp.where(te[:, k : k + 1] == dev_ids, chosen, 0.0)
    logit = logit.astype(BF16)
    for a in range(slabs):
        r_cols = lax.dot_general(
            logit,
            x[:, a * LANES : (a + 1) * LANES],
            (((0,), (0,)), ((), ())),
            preferred_element_type=F32,
        )
        flat[pl.ds(a, n_exp, stride=slabs), :] = r_cols
    rt[...] = flat[pl.ds(0, n_exp * slabs), :].astype(BF16).reshape(rt.shape)

    def rt_out(i, carry):
        d = lax.rem(me + i, n_exp)
        to(rt.at[d], rt_recv.at[me], rt_ss, rt_rs, my, d).start()
        return carry

    lax.fori_loop(1, n_exp, rt_out, 0)
    rt_recv[me] = rt[me]
    wait_for(rt_recv.at[pl.ds(0, others)], rt_rs)
    r2[0] = jnp.sum(rt_recv[...].astype(F32), axis=0)
    for n, d in enumerate((mate, partner, corner)):
        to(r2.at[0], r2.at[n + 1], r2_ss.at[n], r2_rs.at[n], d, me).start()

    wait_for(back.at[pl.ds(0, (2 * n_exp - 1) * cap)], dx_rs)

    def combine(t, carry):
        total = back[place[t * fanout]].astype(F32)
        for k in range(1, fanout):
            total = total + back[place[t * fanout + k]].astype(F32)
        sums[pl.ds(pl.multiple_of(t * slabs, slabs), slabs), :] = total
        return carry

    lax.fori_loop(0, tokens, combine, 0)
    for a in range(slabs):
        cols = slice(a * LANES, (a + 1) * LANES)
        routed = lax.dot_general(
            logit, proj[cols, :], (((1,), (1,)), ((), ())), preferred_element_type=F32
        )
        token_grad[:, cols] = (sums[pl.ds(a, tokens, stride=slabs), :] + routed).astype(BF16)

    for n in range(n_dp - 1):
        wait_for(r2.at[n + 1], r2_rs.at[n])
    rcol[...] = r2[0] + r2[1] + r2[2] + r2[3]
    for n in range(2):
        part = pl.ds(n * half, half)
        wait_for(from_partner.at[part], g_rs.at[3 + n])
    dw[other_slot] = from_partner[...].astype(F32)
    wait_for(from_mate2, g_rs.at[2])
    dw[slot] = dwp[my].astype(F32) + from_mate2[...].astype(F32)

    for n, part in enumerate((x_part, g_part)):
        for t in range(steps):
            wait_for(block.at[part if t == steps - 1 else whole], ring_ss.at[n, t])
    wait_for(table.at[pl.ds(0, n_z - 1)], table_ss)
    wait_for(q_table.at[pl.ds(0, n_z - 1)], qt_ss)
    wait_for(q_all.at[pl.ds(0, sides - 1)], q_ss)
    for rel in range(n_z):
        wait_for(recv.at[rel, pl.ds(0, sides - 1)], tok_ss)
    for n in range(3):
        wait_for(wf.at[0], w_ss.at[n])
    for n in (0, 1, 3, 4):
        wait_for(from_mate.at[pl.ds(0, half)], g_ss.at[n])
    wait_for(from_mate2, g_ss.at[2])
    wait_for(back.at[pl.ds(0, (2 * n_exp - 1) * cap)], dx_ss)
    wait_for(pg_recv.at[pl.ds(0, 2 * n_exp - 1)], pg_ss)
    wait_for(rt.at[pl.ds(0, others)], rt_ss)
    for n in range(n_dp - 1):
        wait_for(r2.at[0], r2_ss.at[n])


def exchange(n_dp, n_exp, place, block, table, q_table, w, x, proj, te, dev, lane, probs):
    slots, quarter, wide = w.shape
    cap = CAP
    slabs = block.shape[1]
    n_z = table.shape[0]
    sides = 2 * n_exp // n_z
    group = sides * cap
    rows = n_z * group
    ff = wide // 3
    tokens, width = x.shape
    vmem = pl.BlockSpec(memory_space=pltpu.VMEM)
    hbm = pl.BlockSpec(memory_space=pl.ANY)
    smem = pl.BlockSpec(memory_space=pltpu.SMEM)
    dma = pltpu.SemaphoreType.DMA
    return pl.pallas_call(
        functools.partial(exchange_kernel, n_dp, n_exp),
        out_shape=(
            jax.ShapeDtypeStruct((tokens, width), BF16),
            jax.ShapeDtypeStruct((slots, quarter, wide), F32),
            jax.ShapeDtypeStruct((slabs, LANES), F32),
        ),
        in_specs=[smem, vmem, vmem, vmem, hbm] + [vmem] * 6,
        out_specs=(vmem, vmem, vmem),
        scratch_shapes=[
            pltpu.VMEM((n_z, sides, 2 * cap, slabs, LANES), BF16),
            pltpu.VMEM((n_z, sides, 2 * cap, slabs, LANES), BF16),
            pltpu.VMEM((n_z, sides, cap, slabs, LANES), BF16),
            pltpu.VMEM((2 * n_exp * cap + 1, slabs, LANES), BF16),
            pltpu.VMEM((n_z, 1, LANES), jnp.int32),
            pltpu.SMEM((n_z, 1, LANES), jnp.int32),
            pltpu.VMEM((n_z, 1, LANES), F32),
            pltpu.VMEM((sides, n_z, 1, LANES), F32),
            pltpu.VMEM((n_dp, quarter, wide), BF16),
            pltpu.VMEM((max(group, n_exp) * slabs, LANES), F32),
            pltpu.VMEM((n_dp, rows, quarter), BF16),
            pltpu.VMEM((n_dp, rows, quarter), BF16),
            pltpu.VMEM((rows, 2 * ff), BF16),
            pltpu.VMEM((rows, ff), BF16),
            pltpu.VMEM((rows, LANES), F32),
            pltpu.VMEM((n_dp, quarter, wide), BF16),
            pltpu.VMEM((quarter, wide), BF16),
            pltpu.VMEM((quarter, wide), BF16),
            pltpu.VMEM((quarter, wide), BF16),
            pltpu.VMEM((n_z, sides, 1, LANES), F32),
            pltpu.VMEM((2 * n_exp, 1, LANES), F32),
            pltpu.VMEM((n_exp, slabs, LANES), BF16),
            pltpu.VMEM((n_exp, slabs, LANES), BF16),
            pltpu.VMEM((n_dp, slabs, LANES), F32),
            pltpu.VMEM((tokens * slabs, LANES), F32),
            dma((2, n_z // 2)),
            dma((2, n_z // 2)),
            dma,
            dma,
            dma,
            dma,
            dma,
            dma,
            dma,
            dma((n_z,)),
            dma((3,)),
            dma((3,)),
            dma((5,)),
            dma((5,)),
            dma,
            dma,
            dma,
            dma,
            dma,
            dma,
            dma((n_dp - 1,)),
            dma((n_dp - 1,)),
            dma((2,)),
        ]
        + [pltpu.VMEM(block.shape, BF16)] * (n_z - 1),
        compiler_params=pltpu.CompilerParams(
            collective_id=0, has_side_effects=True, vmem_limit_bytes=60 * 1024 * 1024
        ),
    )(place, block, table, q_table, w, x, proj, te, dev, lane, probs)


def shards(
    n_dp,
    n_exp,
    layer_inputs,
    output_adjoint,
    dispatcher_projection,
    gating_kernel,
    expansion_kernel,
    contraction_kernel,
    token_experts,
    copy_choice_index,
    expert_copies,
    send_quotas,
):
    tokens, width = layer_inputs.shape
    fanout = token_experts.shape[1]
    experts = dispatcher_projection.shape[1]
    replicas = expert_copies.shape[1]
    position_count = send_quotas.shape[0]
    slots = gating_kernel.shape[1]
    hidden = gating_kernel.shape[2]
    slabs = width // LANES
    pairs = tokens * fanout
    sent = slots * n_exp * CAP

    logits = jnp.dot(layer_inputs, dispatcher_projection, preferred_element_type=F32)
    route_hit = token_experts[:, :, None] == lax.iota(jnp.int32, experts)[None, None, :]
    chosen = jnp.sum(jnp.where(route_hit, logits[:, None, :], 0.0), axis=2)
    probs = jax.nn.softmax(chosen, axis=1)
    flat_pick = (token_experts * replicas + copy_choice_index).reshape(pairs)
    target = jnp.sum(
        jnp.where(
            flat_pick[:, None] == lax.iota(jnp.int32, experts * replicas)[None, :],
            expert_copies.reshape(experts * replicas)[None, :],
            0,
        ),
        axis=1,
    )
    agrees = (target[:, None] == lax.iota(jnp.int32, position_count)[None, :]).astype(jnp.int32)
    arrival = jnp.sum((jnp.cumsum(agrees, axis=0) - agrees) * agrees, axis=1)
    bound = jnp.sum(agrees * send_quotas[None, :], axis=1)
    kept = arrival < bound
    owner = target // slots
    local = target % slots
    position = jnp.where(kept, (local * n_exp + owner) * CAP + arrival, sent)
    hit = position[None, :] == lax.iota(jnp.int32, sent)[:, None]
    pair_token = lax.iota(jnp.int32, pairs) // fanout
    pick = 2 * tokens - jnp.sum(jnp.where(hit, 2 * tokens - pair_token[None, :], 0), axis=1)
    sent_prob = probs.astype(BF16).astype(F32).reshape(1, pairs)
    prob = jnp.sum(jnp.where(hit, sent_prob, 0.0), axis=1)
    n_z = n_exp // PLANE

    def by_plane(values):
        count = slots * PLANE * CAP
        values = values.reshape(slots, n_z, PLANE, CAP).transpose(1, 2, 0, 3)
        return jnp.pad(values.reshape(n_z, 1, count), ((0, 0), (0, 0), (0, LANES - count)))

    table, q_table = by_plane(pick), by_plane(prob)
    block = pl.pallas_call(
        slab_kernel,
        out_shape=jax.ShapeDtypeStruct((2 * tokens + 1, slabs, LANES), BF16),
        in_specs=[pl.BlockSpec(memory_space=pltpu.VMEM)] * 2,
        out_specs=pl.BlockSpec(memory_space=pltpu.VMEM),
        scratch_shapes=[pltpu.VMEM((tokens * slabs, LANES), F32)],
        compiler_params=pltpu.CompilerParams(vmem_limit_bytes=40 * 1024 * 1024),
    )(layer_inputs, output_adjoint)

    weights = jnp.concatenate(
        [gating_kernel, expansion_kernel, contraction_kernel], axis=2
    ).transpose(1, 0, 2)
    device = jnp.where(kept, owner, -1).reshape(tokens, fanout)
    lane = (local * CAP + arrival).reshape(tokens, fanout)
    token_grad, dw, router = exchange(
        n_dp,
        n_exp,
        position,
        block,
        table,
        q_table,
        weights,
        layer_inputs,
        dispatcher_projection,
        token_experts,
        device,
        lane,
        probs,
    )
    dw = dw.transpose(1, 0, 2)
    gate_grad = dw[:, :, :hidden]
    up_grad = dw[:, :, hidden : 2 * hidden]
    down_grad = dw[:, :, 2 * hidden :]
    share = width // n_dp
    router_grad = lax.dynamic_slice(
        router.reshape(width), (lax.axis_index("dp") * share,), (share,)
    )[:, None]
    return (token_grad, gate_grad, up_grad, down_grad, router_grad)


def solution(mesh):
    return jax.shard_map(
        functools.partial(shards, mesh.shape["dp"], mesh.shape["expert"]),
        mesh=mesh,
        in_specs=(
            P(("dp", "expert"), None),
            P(("dp", "expert"), None),
            P(),
            P("dp", "expert", None),
            P("dp", "expert", None),
            P("dp", "expert", None),
            P(("dp", "expert"), None),
            P(("dp", "expert"), None),
            P(),
            P(),
        ),
        out_specs=(
            P(("dp", "expert"), None),
            P("dp", "expert", None),
            P("dp", "expert", None),
            P("dp", "expert", None),
            P("dp", "expert"),
        ),
        check_vma=False,
    )
```

time: 234 us -> 220 us (0.940)
  Pallas kernels: 207 us -> 194 us
    pallas_call x1, Pallas kernels: 202 us -> 193 us  [exchange(): pl.pallas_call(functools.partial(exchange_kernel, n_dp, n_exp), out_shape...]
    pallas_call x1 -> x0, Pallas kernels: 3.98 us -> none  [shards(): pl.pallas_call(combine_kernel, out_shape=jax.ShapeDtypeStruct((tokens, wi...]
    unnamed x31 -> x32, local copies, waits for them, and re-layouts: 12.8 us -> 11.7 us
where the time goes in v2:
time: 220 us
  Pallas kernels  194 us (88%)
  local copies, waits for them, and re-layouts  18.6 us (8%)
  other arithmetic  5.79 us (3%)
    pallas_call x1, Pallas kernels, exchange(): pl.pallas_call(functools.partial(exchange_kernel, n_dp, n_exp), out_shape...  193 us
    unnamed x32, local copies, waits for them, and re-layouts  11.7 us

profile of v2, /device:TPU:1, one launch (start us, length us, event | category | flops | bytes accessed | tf_op | source)
XLA Modules:
  0.0 219.8 jit_solution(166111176348787617)
XLA Ops:
  0.7 0.8 multiply_add_fusion
  1.5 0.1 copy.61
  1.7 0.8 copy.62
  2.4 0.1 broadcast_in_dim.70
  2.5 0.4 select_reduce_fusion.2
  2.9 0.1 copy.63
  3.0 0.2 fusion.2
  3.3 0.1 copy.64
  3.4 0.5 select_reduce_fusion.3
  4.0 0.3 select_reduce_fusion.1
  4.3 0.2 sub.56
  4.6 0.1 reshape.136
  4.7 0.6 pad.8.table
  5.3 0.3 fusion.25
  5.8 0.7 convert_convert_fusion
  6.7 0.3 select_reduce_fusion
  7.0 0.2 reshape.137
  7.3 0.1 reshape.138
  7.4 0.6 pad.9.q_table
  8.3 0.7 fusion.7
  9.3 1.6 maximum_bitcast_fusion.w
  11.0 1.1 shard_map.137.block
  12.2 1.0 copy-done.1
  13.1 1.0 copy.73.proj
  14.1 0.7 copy.74.te
  14.8 193.1 %shard_map.138 = (bf16[128,2048]{1,0:T(8,128)(2,1)}, f32[2,512,1152]{2,1,0:T(8,128)}, f32[16,128]{1,0:T(8,128)}) custom-call(s32[1024]{0:T(1024)} %copy-done.8, bf16[257,16,128]{2,1,0:T(8,128)(2,1)} %copy-done.1, s32[8,1,128]{2,1,0:T(1,128)} %pad.8.table, f32[8,1,128]{2,1,0:T(1,128)} %pad.9.q_table, bf16[2,512,1152]{2,1,0:T(8,128)(2,1)} %maximum_bitcast_fusion.w, ...), custom_call_target="tpu_custom_call" | custom-call | tf_op jit(solution)/shard_map/pallas_call | solution.py:520
  207.9 2.7 %fusion.24 = (f32[512,2,384]{2,0,1:T(8,128)S(1)}, f32[512,2,384]{2,0,1:T(8,128)S(1)}, f32[512,2,384]{2,0,1:T(8,128)S(1)}) fusion(f32[512,2,1152]{2,0,1:T(8,128)} %bitcast.22), kind=kLoop, calls=%fused_computation.59 | loop fusion | bytes 9437184 | tf_op jit(solution)/shard_map/slice | solution.py:676
  210.6 2.4 %copy.75 = f32[512,2,384]{2,1,0:T(2,128)} copy(f32[512,2,384]{2,0,1:T(8,128)S(1)} %get-tuple-element.39) | data formatting | bytes 3145728
  213.0 2.4 %copy.76 = f32[512,2,384]{2,1,0:T(2,128)} copy(f32[512,2,384]{2,0,1:T(8,128)S(1)} %get-tuple-element.38) | data formatting | bytes 3145728
  215.3 2.4 %copy.77 = f32[512,2,384]{2,1,0:T(2,128)} copy(f32[512,2,384]{2,0,1:T(8,128)S(1)} %get-tuple-element.37) | data formatting | bytes 3145728
  217.7 1.3 dynamic_slice.3
  219.0 0.8 copy.79
  (41 shorter events, 1.2 us)
Async XLA Ops:
  0.6 5.0 %copy-start.9 = (s32[128,8]{0,1:T(8,128)S(1)}, s32[128,8]{0,1:T(8,128)}, u32[]{:S(2)}) copy-start(s32[128,8]{0,1:T(8,128)} %param.16) | copy-start | bytes 12292
  0.6 2.8 %copy-start.10 = (s32[128]{0:T(128)S(1)}, s32[128]{0:T(128)}, u32[]{:S(2)}) copy-start(s32[128]{0:T(128)} %param.19) | copy-start | bytes 1540
  0.7 4.7 %copy-start = (bf16[128,2048]{1,0:T(8,128)(2,1)S(1)}, bf16[128,2048]{1,0:T(8,128)(2,1)}, u32[]{:S(2)}) copy-start(bf16[128,2048]{1,0:T(8,128)(2,1)} %x.5) | copy-start | bytes 1572868
  0.7 4.7 %copy-start.3 = (bf16[2048,64]{0,1:T(8,128)(2,1)S(1)}, bf16[2048,64]{0,1:T(8,128)(2,1)}, u32[]{:S(2)}) copy-start(bf16[2048,64]{0,1:T(8,128)(2,1)} %param.12) | copy-start | bytes 786436
  3.2 5.8 %copy-start.4 = (bf16[512,2,384]{2,1,0:T(2,128)(2,1)S(1)}, bf16[512,2,384]{2,1,0:T(2,128)(2,1)}, u32[]{:S(2)}) copy-start(bf16[512,2,384]{2,1,0:T(2,128)(2,1)} %param.13) | copy-start | bytes 2359300
  3.3 5.8 %copy-start.5 = (bf16[512,2,384]{2,1,0:T(2,128)(2,1)S(1)}, bf16[512,2,384]{2,1,0:T(2,128)(2,1)}, u32[]{:S(2)}) copy-start(bf16[512,2,384]{2,1,0:T(2,128)(2,1)} %param.14) | copy-start | bytes 2359300
  4.0 5.2 %copy-start.8 = (s32[1024]{0:T(1024)}, s32[1024]{0:T(1024)S(1)}, u32[]{:S(2)}) copy-start(s32[1024]{0:T(1024)S(1)} %get-tuple-element.42.place) | copy-start | bytes 12292
  4.7 4.5 %copy-start.6 = (bf16[512,2,384]{2,1,0:T(2,128)(2,1)S(1)}, bf16[512,2,384]{2,1,0:T(2,128)(2,1)}, u32[]{:S(2)}) copy-start(bf16[512,2,384]{2,1,0:T(2,128)(2,1)} %param.15) | copy-start | bytes 2359300
  9.3 1.7 copy-start.2
  12.1 1.0 copy-start.1
  213.0 6.0 %copy-start.7 = (bf16[128,2048]{1,0:T(8,128)(2,1)S(1)}, bf16[128,2048]{1,0:T(8,128)(2,1)}, u32[]{:S(2)}) copy-start(bf16[128,2048]{1,0:T(8,128)(2,1)} %get-tuple-element.49) | copy-start | bytes 1572868

commit v3 on v2

--- a/solution.py
+++ b/solution.py
@@ -15,35 +15,26 @@
 BF16 = jnp.bfloat16
 
 
-def slab_kernel(x_ref, g_ref, out_ref, flat):
-    tokens, width = x_ref.shape
-    slabs = width // LANES
-    for which, ref in enumerate((x_ref, g_ref)):
-        for a in range(slabs):
-            flat[pl.ds(a, tokens, stride=slabs), :] = ref[:, a * LANES : (a + 1) * LANES].astype(F32)
-        out_ref[which * tokens : (which + 1) * tokens] = (
-            flat[...].astype(BF16).reshape(tokens, slabs, LANES)
-        )
-    out_ref[2 * tokens] = jnp.zeros((slabs, LANES), BF16)
-
-
 def exchange_kernel(
     n_dp,
     n_exp,
     place,
-    block,
     table,
     q_table,
     w,
     x,
+    g,
     proj,
     te,
-    dev,
+    plane_of,
     lane,
     probs,
     token_grad,
-    dw,
+    gate_grad,
+    up_grad,
+    down_grad,
     rcol,
+    block,
     recv,
     sb,
     dxs,
@@ -64,6 +55,8 @@
     from_mate2,
     from_partner,
     pg,
+    pg_in,
+    pg_mid,
     pg_recv,
     rt,
     rt_recv,
@@ -87,6 +80,8 @@
     dx_rs,
     pg_ss,
     pg_rs,
+    pm_ss,
+    pm_rs,
     rt_ss,
     rt_rs,
     r2_ss,
@@ -115,6 +110,14 @@
     per = slabs // n_dp
     others = n_exp - 1
 
+    for which, ref in enumerate((x, g)):
+        for a in range(slabs):
+            sums[pl.ds(a, tokens, stride=slabs), :] = ref[:, a * LANES : (a + 1) * LANES].astype(F32)
+        block[which * tokens : (which + 1) * tokens] = (
+            sums[...].astype(BF16).reshape(tokens, slabs, LANES)
+        )
+    block[2 * tokens] = jnp.zeros((slabs, LANES), BF16)
+
     barrier = pltpu.get_barrier_semaphore()
 
     def greet(d, e):
@@ -141,26 +144,31 @@
     def wait_for(ref, sem):
         pltpu.make_async_copy(ref, ref, sem).wait()
 
-    whole, x_part, g_part = pl.ds(0, 2 * tokens), pl.ds(0, tokens), pl.ds(tokens, tokens)
+    parts = (pl.ds(0, tokens), pl.ds(tokens, tokens))
     steps = n_z // 2
     up = [block] + list(blocks[: steps - 1])
     down = [block] + list(blocks[steps - 1 : 2 * steps - 2])
     opposite = blocks[2 * steps - 2]
 
-    def ring(t):
-        last = t == steps - 1
-        for n, (held, e, part) in enumerate(((up, above, x_part), (down, below, g_part))):
-            part = part if last else whole
-            target = opposite if last else held[t + 1]
+    def hop(t, n, part):
+        if t == steps - 1:
+            return opposite.at[parts[part]] if part == n else None
+        return (up, down)[n][t + 1].at[parts[part]]
+
+    def ring(t, n, part):
+        target = hop(t, n, part)
+        if target is not None:
+            source = (up, down)[n][t].at[parts[part]]
             to(
-                held[t].at[part], target.at[part], ring_ss.at[n, t], ring_rs.at[n, t], my, e
+                source, target, ring_ss.at[n, t, part], ring_rs.at[n, t, part], my, (above, below)[n]
             ).start()
 
-    def ring_wait(t):
-        last = t == steps - 1
-        for n, (held, part) in enumerate(((up, x_part), (down, g_part))):
-            target = opposite if last else held[t + 1]
-            wait_for(target.at[part if last else whole], ring_rs.at[n, t])
+    def ring_wait(t, n, part):
+        target = hop(t, n, part)
+        if target is not None:
+            wait_for(target, ring_rs.at[n, t, part])
+
+    ways = [(n, part) for part in range(2) for n in range(2)]
 
     def share(rel, held):
         def one(d, carry):
@@ -200,7 +208,8 @@
         lax.fori_loop(1, plane, out, 0)
         recv[rel, inner] = sb[rel, inner]
 
-    ring(0)
+    for n, part in ways:
+        ring(0, n, part)
     to(w.at[slot], wf.at[my], w_ss.at[0], w_rs.at[0], mate, me).start()
     to(w.at[other_slot], wf.at[my], w_ss.at[1], w_rs.at[1], partner, me).start()
     own_w = pltpu.make_async_copy(w.at[slot], wf.at[my], own_sem.at[0])
@@ -296,9 +305,11 @@
         grads = jnp.zeros((sides, LANES), F32)
         for c in range(cap):
             grads = jnp.where(
-                lanes == slot * cap + c, grad[c * sides : (c + 1) * sides], grads
+                lanes == (2 * inner + slot) * cap + c,
+                grad[c * sides : (c + 1) * sides],
+                grads,
             )
-        pg[rel] = grads.reshape(sides, 1, LANES)
+        pg[:, rel] = grads.reshape(sides, 1, LANES)
 
         def expand(p, carry):
             value = lax.dot_general(
@@ -335,10 +346,39 @@
     spot = slot * n_exp + me
     own_rows = pl.ds(spot * cap, cap)
 
-    def pg_start(rel):
-        send_back(rel, pg, pg_recv.at[spot], pg_ss, pg_rs)
-        if rel == 0:
-            pg_recv[spot] = pg[0, inner]
+    def pg_first():
+        def both(i, carry):
+            d = lax.rem(inner + i, plane)
+            for side, y in enumerate((my, partner)):
+                to(
+                    pg.at[side * plane + d],
+                    pg_in.at[side * plane + inner],
+                    pg_ss,
+                    pg_rs,
+                    y,
+                    z * plane + d,
+                ).start()
+            return carry
+
+        to(
+            pg.at[plane + inner], pg_in.at[plane + inner], pg_ss, pg_rs, partner, me
+        ).start()
+        lax.fori_loop(1, plane, both, 0)
+        pg_in[inner] = pg[inner]
+
+    def pg_second():
+        wait_for(pg_in.at[pl.ds(0, sides - 1)], pg_rs)
+        pg_mid[...] = jnp.sum(pg_in[...], axis=0)
+        for rel in range(1, n_z):
+            to(
+                pg_mid.at[rel],
+                pg_recv.at[n_z - rel],
+                pm_ss,
+                pm_rs,
+                my,
+                lax.rem(me + rel * plane, n_exp),
+            ).start()
+        pg_recv[0] = pg_mid[0]
 
     def dx_start(rel):
         send_back(rel, dxs, back.at[own_rows], dx_ss, dx_rs)
@@ -362,86 +402,89 @@
         ).astype(BF16)
 
     share(0, block)
-    done = [0]
+    waiting, done = [0], []
     for t in range(steps - 1):
-        ring_wait(t)
-        ring(t + 1)
+        for n, part in ways:
+            ring_wait(t, n, part)
+            ring(t + 1, n, part)
         if t == 0:
             wait_for(wf.at[partner], w_rs.at[1])
             to(wf.at[partner], wf.at[partner], w_ss.at[2], w_rs.at[2], mate, me).start()
         share(n_z - t - 1, up[t + 1])
         share(t + 1, down[t + 1])
-        if t == steps - 2:
+        if t == max(steps - 3, 0):
             own_w.wait()
             wait_for(wf.at[mate], w_rs.at[0])
             wait_for(wf.at[corner], w_rs.at[2])
             wait_for(q_all.at[pl.ds(0, sides - 1)], q_rs)
-            for rel in done:
+        if t >= steps - 3:
+            for rel in waiting:
                 process(rel)
-                pg_start(rel)
-            last = (n_z - t - 1, t + 1)
-        else:
-            done += [n_z - t - 1, t + 1]
-    ring_wait(steps - 1)
+            done += waiting
+            waiting = []
+        waiting += [n_z - t - 1, t + 1]
+    for n, part in ways:
+        ring_wait(steps - 1, n, part)
     share(steps, opposite)
-    for rel in done:
+    for rel in reversed(done[1:]):
         dx_start(rel)
-    for rel in last:
+    for rel in waiting:
         process(rel)
-        pg_start(rel)
-        dx_start(rel)
     process(steps)
-    pg_start(steps)
+    pg_first()
 
     def give(n, source, target, d):
         to(source, target, g_ss.at[n], g_rs.at[n], d, me).start()
 
+    halves = [pl.ds(n * half, half) for n in range(2)]
+
+    def relay(n):
+        wait_for(from_mate.at[halves[n]], g_rs.at[n])
+        dwp[partner, halves[n]] = (
+            dwp[partner, halves[n]].astype(F32) + from_mate[halves[n]].astype(F32)
+        ).astype(BF16)
+        give(3 + n, dwp.at[partner, halves[n]], from_partner.at[halves[n]], partner)
+
     weight_grad(corner)
     for n in range(2):
-        part = pl.ds(n * half, half)
-        give(n, dwp.at[corner, part], from_mate.at[part], mate)
+        give(n, dwp.at[corner, halves[n]], from_mate.at[halves[n]], mate)
+    for rel in waiting:
+        dx_start(rel)
     dx_start(steps)
     weight_grad(mate)
     give(2, dwp.at[mate], from_mate2, mate)
+    pg_second()
     weight_grad(partner)
-    for n in range(2):
-        part = pl.ds(n * half, half)
-        wait_for(from_mate.at[part], g_rs.at[n])
-        dwp[partner, part] = (
-            dwp[partner, part].astype(F32) + from_mate[part].astype(F32)
-        ).astype(BF16)
-        give(3 + n, dwp.at[partner, part], from_partner.at[part], partner)
+    dx_start(0)
+    relay(0)
     weight_grad(my)
 
-    wait_for(pg_recv.at[pl.ds(0, 2 * n_exp - 1)], pg_rs)
-    grads = pg_recv[...].reshape(2 * n_exp, LANES)
-    grads = (grads[:n_exp] + grads[n_exp:]).astype(BF16)
-    fanout = te.shape[1]
-    dev_ids = lax.broadcasted_iota(jnp.int32, (tokens, n_exp), 1)
-    lane_ids = lax.broadcasted_iota(jnp.int32, (tokens, LANES), 1)
+    wait_for(pg_recv.at[pl.ds(0, n_z - 1)], pm_rs)
+    grads = pg_recv[...].reshape(n_z, LANES).astype(BF16)
+    fanout = te.shape[0]
+    first_dims = (((0,), (0,)), ((), ()))
+    planes = lax.rem(lax.broadcasted_iota(jnp.int32, (n_z, tokens), 0) + z, n_z)
+    spots = lax.broadcasted_iota(jnp.int32, (LANES, tokens), 0)
+    experts = lax.broadcasted_iota(jnp.int32, (n_exp, tokens), 0)
     pair = []
-    weighted = jnp.zeros((tokens, 1), F32)
+    weighted = jnp.zeros((1, tokens), F32)
     for k in range(fanout):
-        hit = (dev[:, k : k + 1] == dev_ids).astype(F32).astype(BF16)
-        spread = jnp.dot(hit, grads, preferred_element_type=F32)
+        hit = (plane_of[k : k + 1, :] == planes).astype(F32).astype(BF16)
+        spread = lax.dot_general(grads, hit, first_dims, preferred_element_type=F32)
         value = jnp.sum(
-            jnp.where(lane[:, k : k + 1] == lane_ids, spread, 0.0), axis=1, keepdims=True
+            jnp.where(lane[k : k + 1, :] == spots, spread, 0.0), axis=0, keepdims=True
         )
         pair.append(value)
-        weighted = weighted + probs[:, k : k + 1] * value
-    logit = jnp.zeros((tokens, n_exp), F32)
+        weighted = weighted + probs[k : k + 1, :] * value
+    logit = jnp.zeros((n_exp, tokens), F32)
     for k in range(fanout):
-        chosen = probs[:, k : k + 1] * (pair[k] - weighted)
-        logit = logit + jnp.where(te[:, k : k + 1] == dev_ids, chosen, 0.0)
+        chosen = probs[k : k + 1, :] * (pair[k] - weighted)
+        logit = logit + jnp.where(te[k : k + 1, :] == experts, chosen, 0.0)
     logit = logit.astype(BF16)
     for a in range(slabs):
-        r_cols = lax.dot_general(
-            logit,
-            x[:, a * LANES : (a + 1) * LANES],
-            (((0,), (0,)), ((), ())),
-            preferred_element_type=F32,
+        flat[pl.ds(a, n_exp, stride=slabs), :] = jnp.dot(
+            logit, x[:, a * LANES : (a + 1) * LANES], preferred_element_type=F32
         )
-        flat[pl.ds(a, n_exp, stride=slabs), :] = r_cols
     rt[...] = flat[pl.ds(0, n_exp * slabs), :].astype(BF16).reshape(rt.shape)
 
     def rt_out(i, carry):
@@ -451,6 +494,7 @@
 
     lax.fori_loop(1, n_exp, rt_out, 0)
     rt_recv[me] = rt[me]
+    relay(1)
     wait_for(rt_recv.at[pl.ds(0, others)], rt_rs)
     r2[0] = jnp.sum(rt_recv[...].astype(F32), axis=0)
     for n, d in enumerate((mate, partner, corner)):
@@ -468,24 +512,29 @@
     lax.fori_loop(0, tokens, combine, 0)
     for a in range(slabs):
         cols = slice(a * LANES, (a + 1) * LANES)
-        routed = lax.dot_general(
-            logit, proj[cols, :], (((1,), (1,)), ((), ())), preferred_element_type=F32
-        )
+        routed = lax.dot_general(logit, proj[:, cols], first_dims, preferred_element_type=F32)
         token_grad[:, cols] = (sums[pl.ds(a, tokens, stride=slabs), :] + routed).astype(BF16)
 
     for n in range(n_dp - 1):
         wait_for(r2.at[n + 1], r2_rs.at[n])
-    rcol[...] = r2[0] + r2[1] + r2[2] + r2[3]
+    sums[pl.ds(0, slabs), :] = r2[0] + r2[1] + r2[2] + r2[3]
+    share_rows = slabs // n_dp
+    rcol[...] = sums[pl.ds(my * share_rows, share_rows), :]
+    outs = (gate_grad, up_grad, down_grad)
     for n in range(2):
-        part = pl.ds(n * half, half)
-        wait_for(from_partner.at[part], g_rs.at[3 + n])
-    dw[other_slot] = from_partner[...].astype(F32)
+        wait_for(from_partner.at[halves[n]], g_rs.at[3 + n])
+    for n, out in enumerate(outs):
+        cols = slice(n * ff, (n + 1) * ff)
+        out[other_slot] = from_partner[:, cols].astype(F32)
     wait_for(from_mate2, g_rs.at[2])
-    dw[slot] = dwp[my].astype(F32) + from_mate2[...].astype(F32)
-
-    for n, part in enumerate((x_part, g_part)):
-        for t in range(steps):
-            wait_for(block.at[part if t == steps - 1 else whole], ring_ss.at[n, t])
+    for n, out in enumerate(outs):
+        cols = slice(n * ff, (n + 1) * ff)
+        out[slot] = dwp[my, :, cols].astype(F32) + from_mate2[:, cols].astype(F32)
+
+    for t in range(steps):
+        for n, part in ways:
+            if hop(t, n, part) is not None:
+                wait_for(block.at[parts[part]], ring_ss.at[n, t, part])
     wait_for(table.at[pl.ds(0, n_z - 1)], table_ss)
     wait_for(q_table.at[pl.ds(0, n_z - 1)], qt_ss)
     wait_for(q_all.at[pl.ds(0, sides - 1)], q_ss)
@@ -497,16 +546,18 @@
         wait_for(from_mate.at[pl.ds(0, half)], g_ss.at[n])
     wait_for(from_mate2, g_ss.at[2])
     wait_for(back.at[pl.ds(0, (2 * n_exp - 1) * cap)], dx_ss)
-    wait_for(pg_recv.at[pl.ds(0, 2 * n_exp - 1)], pg_ss)
+    wait_for(pg_in.at[pl.ds(0, sides - 1)], pg_ss)
+    wait_for(pg_mid.at[pl.ds(0, n_z - 1)], pm_ss)
     wait_for(rt.at[pl.ds(0, others)], rt_ss)
     for n in range(n_dp - 1):
         wait_for(r2.at[0], r2_ss.at[n])
 
 
-def exchange(n_dp, n_exp, place, block, table, q_table, w, x, proj, te, dev, lane, probs):
+def exchange(n_dp, n_exp, place, table, q_table, w, x, g, proj, te, plane_of, lane, probs):
     slots, quarter, wide = w.shape
     cap = CAP
-    slabs = block.shape[1]
+    slabs = x.shape[1] // LANES
+    held = (2 * x.shape[0] + 1, slabs, LANES)
     n_z = table.shape[0]
     sides = 2 * n_exp // n_z
     group = sides * cap
@@ -521,12 +572,15 @@
         functools.partial(exchange_kernel, n_dp, n_exp),
         out_shape=(
             jax.ShapeDtypeStruct((tokens, width), BF16),
-            jax.ShapeDtypeStruct((slots, quarter, wide), F32),
-            jax.ShapeDtypeStruct((slabs, LANES), F32),
+            jax.ShapeDtypeStruct((slots, quarter, ff), F32),
+            jax.ShapeDtypeStruct((slots, quarter, ff), F32),
+            jax.ShapeDtypeStruct((slots, quarter, ff), F32),
+            jax.ShapeDtypeStruct((slabs // n_dp, LANES), F32),
         ),
-        in_specs=[smem, vmem, vmem, vmem, hbm] + [vmem] * 6,
-        out_specs=(vmem, vmem, vmem),
+        in_specs=[smem, vmem, vmem, hbm] + [vmem] * 7,
+        out_specs=(vmem,) * 5,
         scratch_shapes=[
+            pltpu.VMEM(held, BF16),
             pltpu.VMEM((n_z, sides, 2 * cap, slabs, LANES), BF16),
             pltpu.VMEM((n_z, sides, 2 * cap, slabs, LANES), BF16),
             pltpu.VMEM((n_z, sides, cap, slabs, LANES), BF16),
@@ -546,14 +600,16 @@
             pltpu.VMEM((quarter, wide), BF16),
             pltpu.VMEM((quarter, wide), BF16),
             pltpu.VMEM((quarter, wide), BF16),
-            pltpu.VMEM((n_z, sides, 1, LANES), F32),
-            pltpu.VMEM((2 * n_exp, 1, LANES), F32),
+            pltpu.VMEM((sides, n_z, 1, LANES), F32),
+            pltpu.VMEM((sides, n_z, 1, LANES), F32),
+            pltpu.VMEM((n_z, 1, LANES), F32),
+            pltpu.VMEM((n_z, 1, LANES), F32),
             pltpu.VMEM((n_exp, slabs, LANES), BF16),
             pltpu.VMEM((n_exp, slabs, LANES), BF16),
             pltpu.VMEM((n_dp, slabs, LANES), F32),
             pltpu.VMEM((tokens * slabs, LANES), F32),
-            dma((2, n_z // 2)),
-            dma((2, n_z // 2)),
+            dma((2, n_z // 2, 2)),
+            dma((2, n_z // 2, 2)),
             dma,
             dma,
             dma,
@@ -572,15 +628,17 @@
             dma,
             dma,
             dma,
+            dma,
+            dma,
             dma((n_dp - 1,)),
             dma((n_dp - 1,)),
             dma((2,)),
         ]
-        + [pltpu.VMEM(block.shape, BF16)] * (n_z - 1),
+        + [pltpu.VMEM(held, BF16)] * (n_z - 1),
         compiler_params=pltpu.CompilerParams(
             collective_id=0, has_side_effects=True, vmem_limit_bytes=60 * 1024 * 1024
         ),
-    )(place, block, table, q_table, w, x, proj, te, dev, lane, probs)
+    )(place, table, q_table, w, x, g, proj, te, plane_of, lane, probs)
 
 
 def shards(
@@ -641,43 +699,30 @@
         return jnp.pad(values.reshape(n_z, 1, count), ((0, 0), (0, 0), (0, LANES - count)))
 
     table, q_table = by_plane(pick), by_plane(prob)
-    block = pl.pallas_call(
-        slab_kernel,
-        out_shape=jax.ShapeDtypeStruct((2 * tokens + 1, slabs, LANES), BF16),
-        in_specs=[pl.BlockSpec(memory_space=pltpu.VMEM)] * 2,
-        out_specs=pl.BlockSpec(memory_space=pltpu.VMEM),
-        scratch_shapes=[pltpu.VMEM((tokens * slabs, LANES), F32)],
-        compiler_params=pltpu.CompilerParams(vmem_limit_bytes=40 * 1024 * 1024),
-    )(layer_inputs, output_adjoint)
-
     weights = jnp.concatenate(
         [gating_kernel, expansion_kernel, contraction_kernel], axis=2
     ).transpose(1, 0, 2)
-    device = jnp.where(kept, owner, -1).reshape(tokens, fanout)
-    lane = (local * CAP + arrival).reshape(tokens, fanout)
-    token_grad, dw, router = exchange(
+    plane_of = jnp.where(kept, owner // PLANE, -1).reshape(tokens, fanout).T
+    lane = (((owner % PLANE) * slots + local) * CAP + arrival).reshape(tokens, fanout).T
+    token_grad, gate_grad, up_grad, down_grad, router = exchange(
         n_dp,
         n_exp,
         position,
-        block,
         table,
         q_table,
         weights,
         layer_inputs,
-        dispatcher_projection,
-        token_experts,
-        device,
+        output_adjoint,
+        dispatcher_projection.T,
+        token_experts.T,
+        plane_of,
         lane,
-        probs,
+        probs.T,
     )
-    dw = dw.transpose(1, 0, 2)
-    gate_grad = dw[:, :, :hidden]
-    up_grad = dw[:, :, hidden : 2 * hidden]
-    down_grad = dw[:, :, 2 * hidden :]
-    share = width // n_dp
-    router_grad = lax.dynamic_slice(
-        router.reshape(width), (lax.axis_index("dp") * share,), (share,)
-    )[:, None]
+    gate_grad, up_grad, down_grad = (
+        grad.transpose(1, 0, 2) for grad in (gate_grad, up_grad, down_grad)
+    )
+    router_grad = router.reshape(width // n_dp, 1)
     return (token_grad, gate_grad, up_grad, down_grad, router_grad)
 
 

time: 220 us -> 215 us (0.977)
  local copies, waits for them, and re-layouts: 18.6 us -> 14.2 us
    slice x1 -> x0, local copies, waits for them, and re-layouts: 2.68 us -> none  [shards(): down_grad = dw[:, :, 2 * hidden:]]
    unnamed x32 -> x27, local copies, waits for them, and re-layouts: 11.7 us -> 11.1 us
where the time goes in v3:
time: 215 us
  Pallas kernels  192 us (89%)
  local copies, waits for them, and re-layouts  14.2 us (7%)
  other arithmetic  6.18 us (3%)
    pallas_call x1, Pallas kernels, exchange(): pl.pallas_call(functools.partial(exchange_kernel, n_dp, n_exp), out_shape...  192 us
    unnamed x27, local copies, waits for them, and re-layouts  11.1 us

profile of v3, /device:TPU:1, one launch (start us, length us, event | category | flops | bytes accessed | tf_op | source)
XLA Modules:
  0.0 214.7 jit_solution(1067600463715912531)
XLA Ops:
  0.6 0.7 multiply_add_fusion
  1.4 0.8 copy.48
  2.1 0.1 broadcast_in_dim.67
  2.2 1.4 fusion.32
  3.6 0.7 select_reduce_fusion.4
  4.4 0.6 fusion.31
  5.0 0.1 copy.47
  5.2 0.4 select_reduce_fusion.2
  5.6 0.1 copy.49
  5.8 0.1 copy.53
  6.1 0.2 fusion.2
  6.4 0.1 copy.50
  6.5 0.5 select_reduce_fusion.3
  7.0 0.3 select_reduce_fusion.1
  7.4 0.3 select_reduce_fusion
  7.7 0.2 reshape.137
  8.0 0.1 reshape.138
  8.1 0.6 pad.9.q_table
  8.7 0.2 sub.62
  9.0 0.1 reshape.136
  9.1 0.6 pad.8.table
  9.9 0.1 reduce_sum.76
  10.0 0.6 fusion.17
  10.8 0.1 copy.57
  10.9 0.1 copy.58
  11.0 1.6 maximum_bitcast_fusion.w
  12.6 192.0 %shard_map.137 = (bf16[128,2048]{1,0:T(8,128)(2,1)}, f32[2,512,384]{2,1,0:T(8,128)}, f32[2,512,384]{2,1,0:T(8,128)}, f32[2,512,384]{2,1,0:T(8,128)}, f32[4,128]{1,0:T(4,128)}) custom-call(s32[1024]{0:T(1024)} %copy-done.6, s32[8,1,128]{2,1,0:T(1,128)} %pad.8.table, f32[8,1,128]{2,1,0:T(1,128)} %pad.9.q_table, bf16[2,512,1152]{2,1,0:T(8,128)(2,1)} %maximum_bitcast_fusion.w, ...), custom_call_target="tpu_custom_call" | custom-call | tf_op jit(solution)/shard_map/pallas_call | solution.py:571
  204.7 3.9 %copy.66 = f32[512,2,384]{2,1,0:T(2,128)} copy(f32[512,2,384]{2,0,1:T(8,128)} %bitcast.33) | data formatting | bytes 3145728
  208.6 2.4 %copy.67 = f32[512,2,384]{2,1,0:T(2,128)} copy(f32[512,2,384]{2,0,1:T(8,128)S(1)} %bitcast.32) | data formatting | bytes 3145728
  210.9 2.4 %copy.68 = f32[512,2,384]{2,1,0:T(2,128)} copy(f32[512,2,384]{2,0,1:T(8,128)S(1)} %bitcast.31) | data formatting | bytes 3145728
  213.3 0.8 copy.71
  214.1 0.6 copy.72
  (36 shorter events, 0.9 us)
Async XLA Ops:
  0.6 5.8 %copy-start.8 = (s32[128]{0:T(128)S(1)}, s32[128]{0:T(128)}, u32[]{:S(2)}) copy-start(s32[128]{0:T(128)} %param.19) | copy-start | bytes 1540
  4.4 6.3 %copy-start.2 = (bf16[512,2,384]{2,1,0:T(2,128)(2,1)S(1)}, bf16[512,2,384]{2,1,0:T(2,128)(2,1)}, u32[]{:S(2)}) copy-start(bf16[512,2,384]{2,1,0:T(2,128)(2,1)} %param.13) | copy-start | bytes 2359300
  6.3 4.5 %copy-start.3 = (bf16[512,2,384]{2,1,0:T(2,128)(2,1)S(1)}, bf16[512,2,384]{2,1,0:T(2,128)(2,1)}, u32[]{:S(2)}) copy-start(bf16[512,2,384]{2,1,0:T(2,128)(2,1)} %param.14) | copy-start | bytes 2359300
  6.5 4.4 %copy-start.4 = (bf16[512,2,384]{2,1,0:T(2,128)(2,1)S(1)}, bf16[512,2,384]{2,1,0:T(2,128)(2,1)}, u32[]{:S(2)}) copy-start(bf16[512,2,384]{2,1,0:T(2,128)(2,1)} %param.15) | copy-start | bytes 2359300
  7.0 4.0 %copy-start.6 = (s32[1024]{0:T(1024)}, s32[1024]{0:T(1024)S(1)}, u32[]{:S(2)}) copy-start(s32[1024]{0:T(1024)S(1)} %get-tuple-element.36.place) | copy-start | bytes 12292
  204.7 3.9 %copy-start.1 = (f32[2,512,384]{2,1,0:T(8,128)S(1)}, f32[2,512,384]{2,1,0:T(8,128)}, u32[]{:S(2)}) copy-start(f32[2,512,384]{2,1,0:T(8,128)} %get-tuple-element.12) | copy-start | bytes 4718596
  208.6 2.4 %copy-start = (f32[2,512,384]{2,1,0:T(8,128)S(1)}, f32[2,512,384]{2,1,0:T(8,128)}, u32[]{:S(2)}) copy-start(f32[2,512,384]{2,1,0:T(8,128)} %get-tuple-element.13) | copy-start | bytes 4718596
  210.9 2.4 %copy-start.5 = (bf16[128,2048]{1,0:T(8,128)(2,1)S(1)}, bf16[128,2048]{1,0:T(8,128)(2,1)}, u32[]{:S(2)}) copy-start(bf16[128,2048]{1,0:T(8,128)(2,1)} %get-tuple-element.43) | copy-start | bytes 1572868
  210.9 3.2 %copy-start.7 = (f32[4,128]{1,0:T(4,128)S(1)}, f32[4,128]{1,0:T(4,128)}, u32[]{:S(2)}) copy-start(f32[4,128]{1,0:T(4,128)} %get-tuple-element.14) | copy-start | bytes 6148

commit v4 on v3

--- a/solution.py
+++ b/solution.py
@@ -18,22 +18,26 @@
 def exchange_kernel(
     n_dp,
     n_exp,
-    place,
-    table,
-    q_table,
     w,
     x,
     g,
     proj,
     te,
-    plane_of,
-    lane,
-    probs,
+    choice,
+    copies,
+    quotas,
     token_grad,
     gate_grad,
     up_grad,
     down_grad,
     rcol,
+    table,
+    q_table,
+    plane_of,
+    lane,
+    probs,
+    spots_of,
+    place,
     block,
     recv,
     sb,
@@ -110,6 +114,22 @@
     per = slabs // n_dp
     others = n_exp - 1
 
+    barrier = pltpu.get_barrier_semaphore()
+
+    def greet(d, e):
+        pl.semaphore_signal(
+            barrier, inc=1, device_id={"dp": d, "expert": e}, device_id_type=MESH
+        )
+
+    def greet_both(i, carry):
+        greet(my, lax.rem(me + i, n_exp))
+        greet(partner, lax.rem(me + i, n_exp))
+        return carry
+
+    greet(mate, me)
+    greet(corner, me)
+    greet(partner, me)
+    lax.fori_loop(1, n_exp, greet_both, 0)
     for which, ref in enumerate((x, g)):
         for a in range(slabs):
             sums[pl.ds(a, tokens, stride=slabs), :] = ref[:, a * LANES : (a + 1) * LANES].astype(F32)
@@ -117,23 +137,6 @@
             sums[...].astype(BF16).reshape(tokens, slabs, LANES)
         )
     block[2 * tokens] = jnp.zeros((slabs, LANES), BF16)
-
-    barrier = pltpu.get_barrier_semaphore()
-
-    def greet(d, e):
-        pl.semaphore_signal(
-            barrier, inc=1, device_id={"dp": d, "expert": e}, device_id_type=MESH
-        )
-
-    def greet_both(i, carry):
-        greet(my, lax.rem(me + i, n_exp))
-        greet(partner, lax.rem(me + i, n_exp))
-        return carry
-
-    greet(mate, me)
-    greet(corner, me)
-    greet(partner, me)
-    lax.fori_loop(1, n_exp, greet_both, 0)
     pl.semaphore_wait(barrier, 2 * n_exp + 1)
 
     def to(src, dst, ss, rs, d, e):
@@ -175,7 +178,7 @@
             for side, s in enumerate((slot, other_slot)):
                 first = (2 * d + s) * cap
                 for c in range(cap):
-                    token = table_smem[rel, 0, first + c]
+                    token = jnp.clip(table_smem[rel, 0, first + c], 0, 2 * tokens)
                     sb[rel, side * plane + d, c] = held[token]
                     sb[rel, side * plane + d, cap + c] = held[
                         jnp.minimum(token + tokens, 2 * tokens)
@@ -208,12 +211,82 @@
         lax.fori_loop(1, plane, out, 0)
         recv[rel, inner] = sb[rel, inner]
 
+    fanout = te.shape[0]
+    last_dims = (((1,), (1,)), ((), ()))
+
+    def route():
+        ids = lambda count: lax.broadcasted_iota(jnp.int32, (count, tokens), 0)
+        flag = lambda hit: hit.astype(F32).astype(BF16)
+        matmul = lambda a, b: jnp.dot(a, b, preferred_element_type=F32)
+        experts, replicas = proj.shape[0], copies.shape[1] // proj.shape[0]
+        logits = lax.dot_general(proj[...], x[...], last_dims, preferred_element_type=F32)
+        chosen = jnp.concatenate(
+            [
+                jnp.sum(
+                    jnp.where(te[k : k + 1, :] == ids(experts), logits, 0.0), axis=0, keepdims=True
+                )
+                for k in range(fanout)
+            ],
+            axis=0,
+        )
+        powers = jnp.exp(chosen - jnp.max(chosen, axis=0, keepdims=True))
+        probs[...] = powers / jnp.sum(powers, axis=0, keepdims=True)
+        slot_row = jnp.broadcast_to(copies[...].astype(F32), (16, copies.shape[1])).astype(BF16)
+        quota_row = jnp.broadcast_to(quotas[...].astype(F32), (16, quotas.shape[1])).astype(BF16)
+        targets, hits = [], []
+        for k in range(fanout):
+            pick = te[k : k + 1, :] * replicas + choice[k : k + 1, :]
+            target = matmul(slot_row, flag(pick == ids(copies.shape[1])))[0:1].astype(jnp.int32)
+            targets.append(target)
+            hits.append(target == ids(quotas.shape[1]))
+        count = sum(hit.astype(F32) for hit in hits).astype(BF16)
+        earlier = lax.broadcasted_iota(jnp.int32, (tokens, tokens), 0) < lax.broadcasted_iota(
+            jnp.int32, (tokens, tokens), 1
+        )
+        ahead = matmul(count, flag(earlier))
+        value = 2 * tokens - lax.broadcasted_iota(jnp.int32, (n_z, tokens), 1)
+        picks = jnp.zeros((n_z, LANES), F32)
+        weights = jnp.zeros((n_z, LANES), F32)
+        n_slots = w.shape[0]
+        for k in range(fanout):
+            arrival = jnp.sum(jnp.where(hits[k], ahead, 0.0), axis=0, keepdims=True)
+            kept = arrival < matmul(quota_row, flag(hits[k]))[0:1]
+            arrival = arrival.astype(jnp.int32)
+            owner, local = lax.div(targets[k], n_slots), lax.rem(targets[k], n_slots)
+            to_plane = jnp.where(kept, lax.div(owner, plane), -1)
+            spot_lane = (lax.rem(owner, plane) * n_slots + local) * cap + arrival
+            plane_of[k : k + 1, :] = to_plane
+            lane[k : k + 1, :] = spot_lane
+            spots_of[k : k + 1, :] = jnp.where(
+                kept, (local * n_exp + owner) * cap + arrival, n_slots * n_exp * cap
+            )
+            there = to_plane == ids(n_z)
+            spread = flag(spot_lane == ids(LANES))
+            picks = picks + lax.dot_general(
+                jnp.where(there, value, 0).astype(F32).astype(BF16),
+                spread,
+                last_dims,
+                preferred_element_type=F32,
+            )
+            weights = weights + lax.dot_general(
+                jnp.where(there, probs[k : k + 1, :], 0.0).astype(BF16),
+                spread,
+                last_dims,
+                preferred_element_type=F32,
+            )
+        picks = jnp.clip(picks, 0.0, 2.0 * tokens).astype(jnp.int32)
+        table[...] = jnp.clip(2 * tokens - picks, 0, 2 * tokens).reshape(table.shape)
+        q_table[...] = weights.reshape(q_table.shape)
+
     for n, part in ways:
         ring(0, n, part)
     to(w.at[slot], wf.at[my], w_ss.at[0], w_rs.at[0], mate, me).start()
     to(w.at[other_slot], wf.at[my], w_ss.at[1], w_rs.at[1], partner, me).start()
     own_w = pltpu.make_async_copy(w.at[slot], wf.at[my], own_sem.at[0])
     own_w.start()
+    route()
+    to_place = pltpu.make_async_copy(spots_of, place, own_sem.at[2])
+    to_place.start()
     for source, target, ss, rs in (
         (table, table_recv, table_ss, table_rs),
         (q_table, q_mid, qt_ss, qt_rs),
@@ -346,6 +419,11 @@
     spot = slot * n_exp + me
     own_rows = pl.ds(spot * cap, cap)
 
+    def dx_start(rel):
+        send_back(rel, dxs, back.at[own_rows], dx_ss, dx_rs)
+        if rel == 0:
+            back[own_rows] = dxs[0, inner]
+
     def pg_first():
         def both(i, carry):
             d = lax.rem(inner + i, plane)
@@ -379,11 +457,6 @@
                 lax.rem(me + rel * plane, n_exp),
             ).start()
         pg_recv[0] = pg_mid[0]
-
-    def dx_start(rel):
-        send_back(rel, dxs, back.at[own_rows], dx_ss, dx_rs)
-        if rel == 0:
-            back[own_rows] = dxs[0, inner]
 
     def weight_grad(p):
         both = (((0,), (0,)), ((), ()))
@@ -461,7 +534,6 @@
 
     wait_for(pg_recv.at[pl.ds(0, n_z - 1)], pm_rs)
     grads = pg_recv[...].reshape(n_z, LANES).astype(BF16)
-    fanout = te.shape[0]
     first_dims = (((0,), (0,)), ((), ()))
     planes = lax.rem(lax.broadcasted_iota(jnp.int32, (n_z, tokens), 0) + z, n_z)
     spots = lax.broadcasted_iota(jnp.int32, (LANES, tokens), 0)
@@ -502,10 +574,15 @@
 
     wait_for(back.at[pl.ds(0, (2 * n_exp - 1) * cap)], dx_rs)
 
+    to_place.wait()
+
     def combine(t, carry):
-        total = back[place[t * fanout]].astype(F32)
+        def row(k):
+            return back[jnp.clip(place[k, t], 0, 2 * n_exp * cap)].astype(F32)
+
+        total = row(0)
         for k in range(1, fanout):
-            total = total + back[place[t * fanout + k]].astype(F32)
+            total = total + row(k)
         sums[pl.ds(pl.multiple_of(t * slabs, slabs), slabs), :] = total
         return carry
 
@@ -553,12 +630,13 @@
         wait_for(r2.at[0], r2_ss.at[n])
 
 
-def exchange(n_dp, n_exp, place, table, q_table, w, x, g, proj, te, plane_of, lane, probs):
+def exchange(n_dp, n_exp, w, x, g, proj, te, choice, copies, quotas):
     slots, quarter, wide = w.shape
     cap = CAP
     slabs = x.shape[1] // LANES
     held = (2 * x.shape[0] + 1, slabs, LANES)
-    n_z = table.shape[0]
+    n_z = n_exp // PLANE
+    fanout = te.shape[0]
     sides = 2 * n_exp // n_z
     group = sides * cap
     rows = n_z * group
@@ -566,7 +644,6 @@
     tokens, width = x.shape
     vmem = pl.BlockSpec(memory_space=pltpu.VMEM)
     hbm = pl.BlockSpec(memory_space=pl.ANY)
-    smem = pl.BlockSpec(memory_space=pltpu.SMEM)
     dma = pltpu.SemaphoreType.DMA
     return pl.pallas_call(
         functools.partial(exchange_kernel, n_dp, n_exp),
@@ -577,9 +654,16 @@
             jax.ShapeDtypeStruct((slots, quarter, ff), F32),
             jax.ShapeDtypeStruct((slabs // n_dp, LANES), F32),
         ),
-        in_specs=[smem, vmem, vmem, hbm] + [vmem] * 7,
+        in_specs=[hbm] + [vmem] * 7,
         out_specs=(vmem,) * 5,
         scratch_shapes=[
+            pltpu.VMEM((n_z, 1, LANES), jnp.int32),
+            pltpu.VMEM((n_z, 1, LANES), F32),
+            pltpu.VMEM((fanout, tokens), jnp.int32),
+            pltpu.VMEM((fanout, tokens), jnp.int32),
+            pltpu.VMEM((fanout, tokens), F32),
+            pltpu.VMEM((fanout, tokens), jnp.int32),
+            pltpu.SMEM((fanout, tokens), jnp.int32),
             pltpu.VMEM(held, BF16),
             pltpu.VMEM((n_z, sides, 2 * cap, slabs, LANES), BF16),
             pltpu.VMEM((n_z, sides, 2 * cap, slabs, LANES), BF16),
@@ -632,13 +716,13 @@
             dma,
             dma((n_dp - 1,)),
             dma((n_dp - 1,)),
-            dma((2,)),
+            dma((3,)),
         ]
         + [pltpu.VMEM(held, BF16)] * (n_z - 1),
         compiler_params=pltpu.CompilerParams(
             collective_id=0, has_side_effects=True, vmem_limit_bytes=60 * 1024 * 1024
         ),
-    )(place, table, q_table, w, x, g, proj, te, plane_of, lane, probs)
+    )(w, x, g, proj, te, choice, copies, quotas)
 
 
 def shards(
@@ -655,69 +739,22 @@
     expert_copies,
     send_quotas,
 ):
-    tokens, width = layer_inputs.shape
-    fanout = token_experts.shape[1]
-    experts = dispatcher_projection.shape[1]
-    replicas = expert_copies.shape[1]
-    position_count = send_quotas.shape[0]
-    slots = gating_kernel.shape[1]
-    hidden = gating_kernel.shape[2]
-    slabs = width // LANES
-    pairs = tokens * fanout
-    sent = slots * n_exp * CAP
-
-    logits = jnp.dot(layer_inputs, dispatcher_projection, preferred_element_type=F32)
-    route_hit = token_experts[:, :, None] == lax.iota(jnp.int32, experts)[None, None, :]
-    chosen = jnp.sum(jnp.where(route_hit, logits[:, None, :], 0.0), axis=2)
-    probs = jax.nn.softmax(chosen, axis=1)
-    flat_pick = (token_experts * replicas + copy_choice_index).reshape(pairs)
-    target = jnp.sum(
-        jnp.where(
-            flat_pick[:, None] == lax.iota(jnp.int32, experts * replicas)[None, :],
-            expert_copies.reshape(experts * replicas)[None, :],
-            0,
-        ),
-        axis=1,
-    )
-    agrees = (target[:, None] == lax.iota(jnp.int32, position_count)[None, :]).astype(jnp.int32)
-    arrival = jnp.sum((jnp.cumsum(agrees, axis=0) - agrees) * agrees, axis=1)
-    bound = jnp.sum(agrees * send_quotas[None, :], axis=1)
-    kept = arrival < bound
-    owner = target // slots
-    local = target % slots
-    position = jnp.where(kept, (local * n_exp + owner) * CAP + arrival, sent)
-    hit = position[None, :] == lax.iota(jnp.int32, sent)[:, None]
-    pair_token = lax.iota(jnp.int32, pairs) // fanout
-    pick = 2 * tokens - jnp.sum(jnp.where(hit, 2 * tokens - pair_token[None, :], 0), axis=1)
-    sent_prob = probs.astype(BF16).astype(F32).reshape(1, pairs)
-    prob = jnp.sum(jnp.where(hit, sent_prob, 0.0), axis=1)
-    n_z = n_exp // PLANE
-
-    def by_plane(values):
-        count = slots * PLANE * CAP
-        values = values.reshape(slots, n_z, PLANE, CAP).transpose(1, 2, 0, 3)
-        return jnp.pad(values.reshape(n_z, 1, count), ((0, 0), (0, 0), (0, LANES - count)))
-
-    table, q_table = by_plane(pick), by_plane(prob)
+    width = layer_inputs.shape[1]
+
     weights = jnp.concatenate(
         [gating_kernel, expansion_kernel, contraction_kernel], axis=2
     ).transpose(1, 0, 2)
-    plane_of = jnp.where(kept, owner // PLANE, -1).reshape(tokens, fanout).T
-    lane = (((owner % PLANE) * slots + local) * CAP + arrival).reshape(tokens, fanout).T
     token_grad, gate_grad, up_grad, down_grad, router = exchange(
         n_dp,
         n_exp,
-        position,
-        table,
-        q_table,
         weights,
         layer_inputs,
         output_adjoint,
         dispatcher_projection.T,
         token_experts.T,
-        plane_of,
-        lane,
-        probs.T,
+        copy_choice_index.T,
+        expert_copies.reshape(1, -1),
+        send_quotas.reshape(1, -1),
     )
     gate_grad, up_grad, down_grad = (
         grad.transpose(1, 0, 2) for grad in (gate_grad, up_grad, down_grad)

time: 215 us -> 207 us (0.963)
  other arithmetic: 6.18 us -> 1.62 us
    unnamed x27 -> x19, local copies, waits for them, and re-layouts: 11.1 us -> 13.4 us
    reduce_sum x6 -> x0, other arithmetic: 2.29 us -> none  [the longest x1 0.73 us: shards(): chosen = jnp.sum(jnp.where(route_hit, logits[:, None, :], 0.0), axis=2)]
where the time goes in v4:
time: 207 us
  Pallas kernels  191 us (92%)
  local copies, waits for them, and re-layouts  14.1 us (7%)
    pallas_call x1, Pallas kernels, exchange(): pl.pallas_call(functools.partial(exchange_kernel, n_dp, n_exp), out_shape...  191 us
    unnamed x19, local copies, waits for them, and re-layouts  13.4 us

profile of v4, /device:TPU:1, one launch (start us, length us, event | category | flops | bytes accessed | tf_op | source)
XLA Modules:
  0.0 207.2 jit_solution(15763832302172929842)
XLA Ops:
  0.6 0.0 copy-start.2
  0.6 0.8 copy.25
  1.5 0.7 reshape.19.copies
  2.2 1.2 copy.22
  3.4 1.2 copy.23
  4.6 0.0 copy-done.2
  4.6 0.1 copy.24
  4.7 1.6 maximum_bitcast_fusion.w
  6.4 190.8 %shard_map.137 = (bf16[128,2048]{1,0:T(8,128)(2,1)}, f32[2,512,384]{2,1,0:T(8,128)}, f32[2,512,384]{2,1,0:T(8,128)}, f32[2,512,384]{2,1,0:T(8,128)}, f32[4,128]{1,0:T(4,128)}) custom-call(bf16[2,512,1152]{2,1,0:T(8,128)(2,1)} %maximum_bitcast_fusion.w, bf16[128,2048]{1,0:T(8,128)(2,1)} %x.1, bf16[128,2048]{1,0:T(8,128)(2,1)} %g.1, ...), custom_call_target="tpu_custom_call" | custom-call | tf_op jit(solution)/shard_map/pallas_call | solution.py:648
  197.2 0.0 copy-start.1
  197.2 0.0 copy-start
  197.2 3.9 %copy.26 = f32[512,2,384]{2,1,0:T(2,128)} copy(f32[512,2,384]{2,0,1:T(8,128)} %bitcast.12) | data formatting | bytes 3145728
  201.1 0.0 copy-done.1
  201.1 2.4 %copy.27 = f32[512,2,384]{2,1,0:T(2,128)} copy(f32[512,2,384]{2,0,1:T(8,128)S(1)} %bitcast.11) | data formatting | bytes 3145728
  203.5 0.0 copy-done
  203.5 0.0 copy-start.3
  203.5 0.0 copy-start.4
  203.5 2.4 %copy.28 = f32[512,2,384]{2,1,0:T(2,128)} copy(f32[512,2,384]{2,0,1:T(8,128)S(1)} %bitcast.10) | data formatting | bytes 3145728
  205.9 0.0 copy-done.3
  205.9 0.8 copy.31
  206.6 0.0 copy-done.4
  206.6 0.6 copy.32
Async XLA Ops:
  0.6 4.0 %copy-start.2 = (bf16[512,2,384]{2,1,0:T(2,128)(2,1)S(1)}, bf16[512,2,384]{2,1,0:T(2,128)(2,1)}, u32[]{:S(2)}) copy-start(bf16[512,2,384]{2,1,0:T(2,128)(2,1)} %param.15) | copy-start | bytes 2359300
  197.2 3.9 %copy-start.1 = (f32[2,512,384]{2,1,0:T(8,128)S(1)}, f32[2,512,384]{2,1,0:T(8,128)}, u32[]{:S(2)}) copy-start(f32[2,512,384]{2,1,0:T(8,128)} %get-tuple-element.12) | copy-start | bytes 4718596
  197.2 6.3 %copy-start = (f32[2,512,384]{2,1,0:T(8,128)S(1)}, f32[2,512,384]{2,1,0:T(8,128)}, u32[]{:S(2)}) copy-start(f32[2,512,384]{2,1,0:T(8,128)} %get-tuple-element.13) | copy-start | bytes 4718596
  203.5 2.4 %copy-start.3 = (bf16[128,2048]{1,0:T(8,128)(2,1)S(1)}, bf16[128,2048]{1,0:T(8,128)(2,1)}, u32[]{:S(2)}) copy-start(bf16[128,2048]{1,0:T(8,128)(2,1)} %get-tuple-element.30) | copy-start | bytes 1572868
  203.5 3.2 %copy-start.4 = (f32[4,128]{1,0:T(4,128)S(1)}, f32[4,128]{1,0:T(4,128)}, u32[]{:S(2)}) copy-start(f32[4,128]{1,0:T(4,128)} %get-tuple-element.14) | copy-start | bytes 6148

commit v5 on v4

--- a/solution.py
+++ b/solution.py
@@ -586,7 +586,7 @@
         sums[pl.ds(pl.multiple_of(t * slabs, slabs), slabs), :] = total
         return carry
 
-    lax.fori_loop(0, tokens, combine, 0)
+    lax.fori_loop(0, tokens, combine, 0, unroll=4)
     for a in range(slabs):
         cols = slice(a * LANES, (a + 1) * LANES)
         routed = lax.dot_general(logit, proj[:, cols], first_dims, preferred_element_type=F32)

time: 207 us -> 207 us (level)
  no operation moved by 1% of the time
where the time goes in v5:
time: 207 us
  Pallas kernels  191 us (92%)
  local copies, waits for them, and re-layouts  14.1 us (7%)
    pallas_call x1, Pallas kernels, exchange(): pl.pallas_call(functools.partial(exchange_kernel, n_dp, n_exp), out_shape...  191 us
    unnamed x19, local copies, waits for them, and re-layouts  13.4 us

profile of v5, /device:TPU:1, one launch (start us, length us, event | category | flops | bytes accessed | tf_op | source)
XLA Modules:
  0.0 207.2 jit_solution(5288380381446186958)
XLA Ops:
  0.6 0.0 copy-start.2
  0.6 0.8 copy.25
  1.5 0.7 reshape.19.copies
  2.2 1.2 copy.22
  3.4 1.2 copy.23
  4.6 0.0 copy-done.2
  4.6 0.1 copy.24
  4.7 1.6 maximum_bitcast_fusion.w
  6.4 190.8 %shard_map.137 = (bf16[128,2048]{1,0:T(8,128)(2,1)}, f32[2,512,384]{2,1,0:T(8,128)}, f32[2,512,384]{2,1,0:T(8,128)}, f32[2,512,384]{2,1,0:T(8,128)}, f32[4,128]{1,0:T(4,128)}) custom-call(bf16[2,512,1152]{2,1,0:T(8,128)(2,1)} %maximum_bitcast_fusion.w, bf16[128,2048]{1,0:T(8,128)(2,1)} %x.1, bf16[128,2048]{1,0:T(8,128)(2,1)} %g.1, ...), custom_call_target="tpu_custom_call" | custom-call | tf_op jit(solution)/shard_map/pallas_call | solution.py:648
  197.2 0.0 copy-start.1
  197.2 0.0 copy-start
  197.2 3.9 %copy.26 = f32[512,2,384]{2,1,0:T(2,128)} copy(f32[512,2,384]{2,0,1:T(8,128)} %bitcast.12) | data formatting | bytes 3145728
  201.1 0.0 copy-done.1
  201.1 2.4 %copy.27 = f32[512,2,384]{2,1,0:T(2,128)} copy(f32[512,2,384]{2,0,1:T(8,128)S(1)} %bitcast.11) | data formatting | bytes 3145728
  203.5 0.0 copy-done
  203.5 0.0 copy-start.3
  203.5 0.0 copy-start.4
  203.5 2.4 %copy.28 = f32[512,2,384]{2,1,0:T(2,128)} copy(f32[512,2,384]{2,0,1:T(8,128)S(1)} %bitcast.10) | data formatting | bytes 3145728
  205.9 0.0 copy-done.3
  205.9 0.8 copy.31
  206.6 0.0 copy-done.4
  206.6 0.6 copy.32
Async XLA Ops:
  0.6 4.0 %copy-start.2 = (bf16[512,2,384]{2,1,0:T(2,128)(2,1)S(1)}, bf16[512,2,384]{2,1,0:T(2,128)(2,1)}, u32[]{:S(2)}) copy-start(bf16[512,2,384]{2,1,0:T(2,128)(2,1)} %param.15) | copy-start | bytes 2359300
  197.2 3.9 %copy-start.1 = (f32[2,512,384]{2,1,0:T(8,128)S(1)}, f32[2,512,384]{2,1,0:T(8,128)}, u32[]{:S(2)}) copy-start(f32[2,512,384]{2,1,0:T(8,128)} %get-tuple-element.12) | copy-start | bytes 4718596
  197.2 6.3 %copy-start = (f32[2,512,384]{2,1,0:T(8,128)S(1)}, f32[2,512,384]{2,1,0:T(8,128)}, u32[]{:S(2)}) copy-start(f32[2,512,384]{2,1,0:T(8,128)} %get-tuple-element.13) | copy-start | bytes 4718596
  203.5 2.4 %copy-start.3 = (bf16[128,2048]{1,0:T(8,128)(2,1)S(1)}, bf16[128,2048]{1,0:T(8,128)(2,1)}, u32[]{:S(2)}) copy-start(bf16[128,2048]{1,0:T(8,128)(2,1)} %get-tuple-element.30) | copy-start | bytes 1572868
  203.5 3.2 %copy-start.4 = (f32[4,128]{1,0:T(4,128)S(1)}, f32[4,128]{1,0:T(4,128)}, u32[]{:S(2)}) copy-start(f32[4,128]{1,0:T(4,128)} %get-tuple-element.14) | copy-start | bytes 6148
